TPU v7x, 32 devices: a whole 2x2x4 slice. The times are simulated.
32 devices in a mesh: rep: 4 (over x, core), shard: 8 (over z, y).
Axes of the slice: x: 2, y: 2, z: 4, core: 2. Of those that a mesh axis runs over, the one named last changes fastest.
Arguments:
- stream: float32 [8192, 768], P(('rep', 'shard')), may hold values from -6 to 6
- prev_logits: float32 [8192, 8], P(('rep', 'shard')), may hold values from -3 to 3
- segments: int32 [32, 256], P(('rep', 'shard')), may hold values from 0 to 3, never falling along the last dimension, each value on 1 to 128 neighbouring positions
- routes: int32 [8192, 2], P(('rep', 'shard')), may hold values from 0 to 7, all different within a row
- claim_order: int32 [32, 256], P(('rep', 'shard')), may hold values from 0 to 255, each once within a row
- out_cotangent: float32 [8192, 768], P(('rep', 'shard')), may hold values from -6 to 6
- first_gain: bfloat16 [768], P('shard'), may hold values from 0.5 to 1.5
- attend_weight: bfloat16 [768, 2304], P('shard'), may hold values from -0.21875 to 0.21875
- output_weight: bfloat16 [768, 768], P('shard'), may hold values from -0.625 to 0.625
- second_gain: bfloat16 [768], P('shard'), may hold values from 0.5 to 1.5
- router_weight: bfloat16 [768, 8], P('shard'), may hold values from -0.15625 to 0.15625
- constant_mix: bfloat16 [768, 4], P('shard'), may hold values from -0.21875 to 0.21875
- constant_vector: bfloat16 [768, 2], P('shard'), may hold values from -6 to 6
- expert_in: bfloat16 [768, 4, 4096], P('shard'), may hold values from -0.21875 to 0.21875
- expert_out: bfloat16 [2048, 4, 768], P('shard'), may hold values from -1 to 1
Outputs:
- result: bfloat16 [8192, 768], P(('rep', 'shard'))
- stream_grad: float32 [8192, 768], P(('rep', 'shard'))
- logits_grad: float32 [8192, 8], P(('rep', 'shard'))
- first_gain_grad: float32 [768], P('shard')
- attend_grad: float32 [768, 2304], P('shard')
- output_grad: float32 [768, 768], P('shard')
- second_gain_grad: float32 [768], P('shard')
- router_grad: float32 [768, 8], P('shard')
- mix_grad: float32 [768, 4], P('shard')
- vector_grad: float32 [768, 2], P('shard')
- expert_in_grad: float32 [768, 4, 4096], P('shard')
- expert_out_grad: float32 [2048, 4, 768], P('shard')
Inputs may be any that keep to these rules, and one draw needn't show every extreme that they name: `segments`: within a row segment numbers never fall. `routes`: the 2 experts of a token differ. `claim_order`: each row holds every number below 256 once.
All inputs are finite; a program needn't handle non-finite values.
Results may differ from a plain program's by a relative error of at most 0.017.
Values may be sent and summed in bfloat16 or wider, within the bound.
No kernel may reach another device: no remote copies, remote signals or barrier semaphores. Data moves between devices by JAX's collectives and lax.ppermute only.
A program may use at most 320 MiB of HBM per device.

v0:
```python
import math

import jax
import jax.numpy as jnp
from jax import lax
from jax.sharding import PartitionSpec as P

H = 12
HD = 64
FF = 2048
E_FFN = 4
NC = 2
NE = 8
CAP = 64


EPSILON = 1e-06
HIGHEST = lax.Precision.HIGHEST


def rotary_tables(length, head_size):
    half = head_size // 2
    position = jnp.arange(length, dtype=jnp.float32)
    frequency = jnp.exp(
        jnp.arange(half, dtype=jnp.float32) * (-2.0 * math.log(10000.0) / head_size)
    )
    angle = position[:, None] * frequency[None, :]
    return (jnp.cos(angle), jnp.sin(angle))


def rotate(values, cosine, sine):
    half = values.shape[-1] // 2
    first = values[..., :half]
    second = values[..., half:]
    cosine = cosine[:, None, :]
    sine = sine[:, None, :]
    return jnp.concatenate(
        [first * cosine - second * sine, second * cosine + first * sine], axis=-1
    )


def rotate_back(grads, cosine, sine):
    half = grads.shape[-1] // 2
    first = grads[..., :half]
    second = grads[..., half:]
    cosine = cosine[:, None, :]
    sine = sine[:, None, :]
    return jnp.concatenate(
        [first * cosine + second * sine, second * cosine - first * sine], axis=-1
    )


def assign_slots(route_row, order_row, experts, capacity):
    tokens = route_row.shape[0]
    top = route_row.shape[1]
    claims = jnp.take(route_row, order_row, axis=0).reshape(-1)
    onehot = (claims[:, None] == jnp.arange(experts, dtype=jnp.int32)[None, :]).astype(jnp.int32)
    before = jnp.cumsum(onehot, axis=0, dtype=jnp.int32) - onehot
    place = jnp.sum(before * onehot, axis=1, dtype=jnp.int32)
    kept = (claims < experts) & (place < capacity)
    target = jnp.where(kept, claims * capacity + place, experts * capacity)
    owner = jnp.repeat(order_row, top)
    by_token = jnp.zeros((tokens, top), jnp.int32).at[order_row].set(target.reshape(tokens, top))
    table = (
        jnp.full((experts * capacity + 1,), tokens, jnp.int32)
        .at[target]
        .set(owner)[: experts * capacity]
    )
    return (by_token, table)


def masked_scores(query_block, key_rows, segment_row, begin, scale):
    count = query_block.shape[0]
    scores = (
        jnp.einsum("qhd,khd->hqk", query_block, key_rows, preferred_element_type=jnp.float32)
        * scale
    )
    query_place = begin + jnp.arange(count)
    key_place = jnp.arange(key_rows.shape[0])
    allowed = (segment_row[:, None] == segment_row[None, :]) & (
        key_place[None, :] <= query_place[:, None]
    )
    return jnp.where(allowed[None], scores, -1e30)


def local(
    stream,
    prev_logits,
    segments,
    routes,
    claim_order,
    out_cotangent,
    first_gain,
    attend_weight,
    output_weight,
    second_gain,
    router_weight,
    constant_mix,
    constant_vector,
    expert_in,
    expert_out,
):
    tokens, width = stream.shape
    scale = 1.0 / math.sqrt(HD)
    segment_row = segments[0]
    order_row = claim_order[0]
    gain_one, attend_full, output_full, gain_two, router_full, mix_full, vector_full = (
        lax.all_gather(first_gain, "shard", axis=0, tiled=True),
        lax.all_gather(attend_weight, "shard", axis=0, tiled=True),
        lax.all_gather(output_weight, "shard", axis=0, tiled=True),
        lax.all_gather(second_gain, "shard", axis=0, tiled=True),
        lax.all_gather(router_weight, "shard", axis=0, tiled=True),
        lax.all_gather(constant_mix, "shard", axis=0, tiled=True),
        lax.all_gather(constant_vector, "shard", axis=0, tiled=True),
    )
    gain_one_f = gain_one.astype(jnp.float32)
    gain_two_f = gain_two.astype(jnp.float32)
    router_f = router_full.astype(jnp.float32)
    mix_f = mix_full.astype(jnp.float32)
    vector_f = vector_full.astype(jnp.float32)
    inverse_one = lax.rsqrt(jnp.mean(stream * stream, axis=-1, keepdims=True) + EPSILON)
    normed = (stream * inverse_one * gain_one_f).astype(jnp.bfloat16)
    projected = jnp.dot(normed, attend_full, preferred_element_type=jnp.float32).reshape(
        tokens, 3, H, HD
    )
    cosine, sine = rotary_tables(tokens, HD)
    queries = rotate(projected[:, 0], cosine, sine).astype(jnp.bfloat16)
    key_rows = rotate(projected[:, 1], cosine, sine).astype(jnp.bfloat16)
    value_rows = projected[:, 2].astype(jnp.bfloat16)
    block = min(512, tokens)
    starts = list(range(0, tokens, block))
    mixed_parts = []
    log_totals = []
    for begin in starts:
        scores = masked_scores(queries, key_rows, segment_row, begin, scale)
        peak = jnp.max(scores, axis=-1, keepdims=True)
        raised = jnp.exp(scores - peak)
        total = jnp.sum(raised, axis=-1, keepdims=True)
        weights = (raised / total).astype(jnp.bfloat16)
        log_totals.append(peak + jnp.log(total))
        mixed_parts.append(
            jnp.einsum("hqk,khd->qhd", weights, value_rows, preferred_element_type=jnp.float32)
        )
    mixed = mixed_parts[0].reshape(tokens, width).astype(jnp.bfloat16)
    hidden = stream + jnp.dot(mixed, output_full, preferred_element_type=jnp.float32)
    inverse_two = lax.rsqrt(jnp.mean(hidden * hidden, axis=-1, keepdims=True) + EPSILON)
    routed_in = (hidden * inverse_two * gain_two_f).astype(jnp.bfloat16)
    routed_f = routed_in.astype(jnp.float32)
    logits = jnp.dot(routed_in, router_full, preferred_element_type=jnp.float32) + prev_logits
    chances = jax.nn.softmax(logits, axis=-1)
    gates = jnp.take_along_axis(chances, routes, axis=1)
    onehot = (routes[:, :, None] == jnp.arange(NE, dtype=jnp.int32)[None, None, :]).astype(
        jnp.float32
    )
    combine = jnp.sum(gates[:, :, None] * onehot, axis=1)
    by_token, table = assign_slots(routes, order_row, E_FFN, CAP)
    padded = jnp.concatenate([routed_in, jnp.zeros((1, width), jnp.bfloat16)], axis=0)
    slot_in = jnp.take(padded, table, axis=0).reshape(E_FFN, CAP, width)
    columns = slot_in
    gate_up = jnp.einsum(
        "ecd,def->ecf",
        columns,
        lax.all_gather(expert_in, "shard", axis=0, tiled=True),
        preferred_element_type=jnp.float32,
    )
    gate_part = gate_up[..., :FF]
    up_part = gate_up[..., FF:]
    sigma = jax.nn.sigmoid(gate_part)
    swish = gate_part * sigma
    activated = (swish * up_part).astype(jnp.bfloat16)
    columns = activated
    slot_out = jnp.einsum(
        "ecf,fej->ecj",
        columns,
        lax.all_gather(expert_out, "shard", axis=0, tiled=True),
        preferred_element_type=jnp.float32,
    )
    padded_out = jnp.concatenate(
        [slot_out.reshape(E_FFN * CAP, width), jnp.zeros((1, width), jnp.float32)], axis=0
    )
    picked = jnp.take(padded_out, by_token, axis=0)
    expert_sum = jnp.sum(gates[:, :, None] * picked, axis=1)
    copy_weight = combine[:, E_FFN + 1 : E_FFN + 2]
    copy_term = copy_weight * routed_f
    mixing = jax.nn.softmax(
        jnp.dot(routed_in, mix_full, preferred_element_type=jnp.float32).reshape(tokens, NC, 2),
        axis=-1,
    )
    constant_out = mixing[..., 0:1] * routed_f[:, None, :] + mixing[..., 1:2] * vector_f.T[None]
    constant_weight = combine[:, E_FFN + 2 :]
    constant_term = jnp.sum(constant_weight[:, :, None] * constant_out, axis=1)
    result = hidden + expert_sum + copy_term + constant_term
    combine_pad = jnp.concatenate([combine, jnp.zeros((1, NE), jnp.float32)], axis=0)
    slot_rows = jnp.take(combine_pad, table, axis=0).reshape(E_FFN, CAP, NE)
    slot_weight = jnp.sum(
        slot_rows[:, :, :E_FFN] * jnp.eye(E_FFN, dtype=jnp.float32)[:, None, :], axis=2
    )
    upstream_pad = jnp.concatenate([out_cotangent, jnp.zeros((1, width), jnp.float32)], axis=0)
    slot_grad = (
        slot_weight[..., None] * jnp.take(upstream_pad, table, axis=0).reshape(E_FFN, CAP, width)
    ).astype(jnp.bfloat16)
    activated_grad = jnp.einsum(
        "ecj,fej->ecf",
        slot_grad,
        lax.all_gather(expert_out, "shard", axis=0, tiled=True),
        preferred_element_type=jnp.float32,
    )
    gate_grad_part = activated_grad * up_part * sigma * (1.0 + gate_part * (1.0 - sigma))
    up_grad_part = activated_grad * swish
    gate_up_grad = jnp.concatenate([gate_grad_part, up_grad_part], axis=-1).astype(jnp.bfloat16)
    slot_in_grad = jnp.einsum(
        "ecf,def->ecd",
        gate_up_grad,
        lax.all_gather(expert_in, "shard", axis=0, tiled=True),
        preferred_element_type=jnp.float32,
    )
    padded_in_grad = jnp.concatenate(
        [slot_in_grad.reshape(E_FFN * CAP, width), jnp.zeros((1, width), jnp.float32)], axis=0
    )
    routed_grad = jnp.sum(jnp.take(padded_in_grad, by_token, axis=0), axis=1)
    expert_gate_grad = jnp.sum(picked * out_cotangent[:, None, :], axis=-1)
    copy_grad = jnp.sum(out_cotangent * routed_f, axis=-1, keepdims=True)
    constant_grad = jnp.sum(out_cotangent[:, None, :] * constant_out, axis=-1)
    other_grad = jnp.concatenate(
        [jnp.zeros((tokens, E_FFN + 1), jnp.float32), copy_grad, constant_grad], axis=1
    )
    gate_grad = expert_gate_grad + jnp.take_along_axis(other_grad, routes, axis=1)
    chance_grad = jnp.sum(onehot * gate_grad[:, :, None], axis=1)
    logit_grad = chances * (chance_grad - jnp.sum(chances * chance_grad, axis=-1, keepdims=True))
    router_term = jnp.einsum("td,te->de", routed_f, logit_grad, precision=HIGHEST)
    routed_grad = routed_grad + jnp.einsum("te,de->td", logit_grad, router_f, precision=HIGHEST)
    each_constant = constant_weight[:, :, None] * out_cotangent[:, None, :]
    routed_grad = routed_grad + jnp.sum(mixing[..., 0:1] * each_constant, axis=1)
    vector_term = jnp.sum(mixing[..., 1:2] * each_constant, axis=0).T
    alpha_grad = jnp.stack(
        [
            jnp.sum(each_constant * routed_f[:, None, :], axis=-1),
            jnp.einsum("tcd,dc->tc", each_constant, vector_f, precision=HIGHEST),
        ],
        axis=-1,
    )
    mix_logit_grad = (
        mixing * (alpha_grad - jnp.sum(mixing * alpha_grad, axis=-1, keepdims=True))
    ).reshape(tokens, 2 * NC)
    mix_term = jnp.einsum("td,tc->dc", routed_f, mix_logit_grad, precision=HIGHEST)
    routed_grad = routed_grad + jnp.einsum("tc,dc->td", mix_logit_grad, mix_f, precision=HIGHEST)
    routed_grad = routed_grad + copy_weight * out_cotangent
    scaled_two = routed_grad * gain_two_f
    second_term = jnp.sum(routed_grad * hidden * inverse_two, axis=0)
    cube_two = inverse_two * inverse_two * inverse_two
    hidden_grad = (
        out_cotangent
        + inverse_two * scaled_two
        - hidden * cube_two * jnp.mean(scaled_two * hidden, axis=-1, keepdims=True)
    )
    attn_grad = hidden_grad.astype(jnp.bfloat16)
    output_term = jnp.einsum("td,tj->dj", mixed, attn_grad, preferred_element_type=jnp.float32)
    mixed_grad = (
        jnp.einsum("tj,dj->td", attn_grad, output_full, preferred_element_type=jnp.float32)
        .astype(jnp.bfloat16)
        .reshape(tokens, H, HD)
    )
    query_parts = []
    key_grad = jnp.zeros((tokens, H, HD), jnp.float32)
    value_grad = jnp.zeros((tokens, H, HD), jnp.float32)
    for number, begin in enumerate(starts):
        scores = masked_scores(queries, key_rows, segment_row, begin, scale)
        weights = jnp.exp(scores - log_totals[number])
        prob_grad = jnp.einsum(
            "qhd,khd->hqk", mixed_grad, value_rows, preferred_element_type=jnp.float32
        )
        score_grad = (
            weights * (prob_grad - jnp.sum(weights * prob_grad, axis=-1, keepdims=True))
        ).astype(jnp.bfloat16)
        query_parts.append(
            jnp.einsum("hqk,khd->qhd", score_grad, key_rows, preferred_element_type=jnp.float32)
            * scale
        )
        key_grad = (
            jnp.einsum("hqk,qhd->khd", score_grad, queries, preferred_element_type=jnp.float32)
            * scale
        )
        value_grad = jnp.einsum(
            "hqk,qhd->khd",
            weights.astype(jnp.bfloat16),
            mixed_grad,
            preferred_element_type=jnp.float32,
        )
    query_grad = rotate_back(query_parts[0], cosine, sine)
    key_grad = rotate_back(key_grad, cosine, sine)
    projected_grad = (
        jnp.stack([query_grad, key_grad, value_grad], axis=1)
        .reshape(tokens, 3 * width)
        .astype(jnp.bfloat16)
    )
    attend_term = jnp.einsum(
        "td,tj->dj", normed, projected_grad, preferred_element_type=jnp.float32
    )
    normed_grad = jnp.einsum(
        "tj,dj->td", projected_grad, attend_full, preferred_element_type=jnp.float32
    )
    scaled_one = normed_grad * gain_one_f
    first_term = jnp.sum(normed_grad * stream * inverse_one, axis=0)
    cube_one = inverse_one * inverse_one * inverse_one
    stream_grad = (
        hidden_grad
        + inverse_one * scaled_one
        - stream * cube_one * jnp.mean(scaled_one * stream, axis=-1, keepdims=True)
    )
    share_first, share_attend, share_output, share_second, share_router, share_mix, share_vector = (
        lax.psum_scatter(first_term, "shard", scatter_dimension=0, tiled=True),
        lax.psum_scatter(attend_term, "shard", scatter_dimension=0, tiled=True),
        lax.psum_scatter(output_term, "shard", scatter_dimension=0, tiled=True),
        lax.psum_scatter(second_term, "shard", scatter_dimension=0, tiled=True),
        lax.psum_scatter(router_term, "shard", scatter_dimension=0, tiled=True),
        lax.psum_scatter(mix_term, "shard", scatter_dimension=0, tiled=True),
        lax.psum_scatter(vector_term, "shard", scatter_dimension=0, tiled=True),
    )
    columns = slot_in
    in_share = lax.psum_scatter(
        jnp.einsum("ecd,ecf->def", columns, gate_up_grad, preferred_element_type=jnp.float32),
        "shard",
        scatter_dimension=0,
        tiled=True,
    )
    columns = activated
    out_share = lax.psum_scatter(
        jnp.einsum("ecf,ecj->fej", columns, slot_grad, preferred_element_type=jnp.float32),
        "shard",
        scatter_dimension=0,
        tiled=True,
    )
    (
        share_first,
        share_attend,
        share_output,
        share_second,
        share_router,
        share_mix,
        share_vector,
        in_share,
        out_share,
    ) = (
        lax.psum(share_first.astype(jnp.bfloat16), "rep").astype(jnp.float32),
        lax.psum(share_attend.astype(jnp.bfloat16), "rep").astype(jnp.float32),
        lax.psum(share_output.astype(jnp.bfloat16), "rep").astype(jnp.float32),
        lax.psum(share_second.astype(jnp.bfloat16), "rep").astype(jnp.float32),
        lax.psum(share_router.astype(jnp.bfloat16), "rep").astype(jnp.float32),
        lax.psum(share_mix.astype(jnp.bfloat16), "rep").astype(jnp.float32),
        lax.psum(share_vector.astype(jnp.bfloat16), "rep").astype(jnp.float32),
        lax.psum(in_share.astype(jnp.bfloat16), "rep").astype(jnp.float32),
        lax.psum(out_share.astype(jnp.bfloat16), "rep").astype(jnp.float32),
    )
    return (
        result.astype(jnp.bfloat16),
        stream_grad,
        logit_grad,
        share_first,
        share_attend,
        share_output,
        share_second,
        share_router,
        share_mix,
        share_vector,
        in_share,
        out_share,
    )


def solution(mesh):
    placed = (
        P(("rep", "shard"), None),
        P(("rep", "shard"), None),
        P(("rep", "shard"), None),
        P(("rep", "shard"), None),
        P(("rep", "shard"), None),
        P(("rep", "shard"), None),
        P("shard"),
        P("shard", None),
        P("shard", None),
        P("shard"),
        P("shard", None),
        P("shard", None),
        P("shard", None),
        P("shard", None, None),
        P("shard", None, None),
    )
    return jax.shard_map(
        local,
        mesh=mesh,
        in_specs=placed,
        out_specs=(
            P(("rep", "shard"), None),
            P(("rep", "shard"), None),
            P(("rep", "shard"), None),
            P("shard"),
            P("shard", None),
            P("shard", None),
            P("shard"),
            P("shard", None),
            P("shard", None),
            P("shard", None),
            P("shard", None, None),
            P("shard", None, None),
        ),
        check_vma=False,
    )
```

profile of v0, /device:TPU:0, one launch (start us, length us, event | category | flops | bytes accessed | tf_op | source)
XLA Modules:
  0.0 3232.6 jit_solution(82910997496972327)
XLA Ops:
  8.7 5.3 copy.172
  14.2 1.2 copy-done.19
  15.4 1.3 copy.173
  16.8 22.2 all-gather.2
  42.8 17.8 all-reduce.11
  60.6 18.2 all-gather.1
  79.5 26.1 all-gather
  107.4 1.2 reduce-window.6
  109.9 1.2 scatter_custom_fusion.1
  111.7 2.7 scatter_custom_fusion
  115.2 2.0 gather_fusion.3
  119.5 3.6 fusion.66
  125.2 1.1 copy-done
  127.1 2.1 multiply_reduce_fusion.13
  131.6 4.0 gather_fusion.4
  136.6 0.9 convert_element_type.143
  141.7 1.2 gather_fusion.1
  143.1 458.8 %all-gather.12.cloned.1.call-done = bf16[768,4,4096]{2,0,1:T(8,128)(2,1)} async-done(((bf16[96,4,4096]{2,0,1:T(8,128)(2,1)}), bf16[768,4,4096]{2,0,1:T(8,128)(2,1)}) %all-gather.12.cloned.1.call-update) | async-done | bytes 25165840 | tf_op jit(solution)/shard_map/all_gather | solution.py:163
  602.0 14.7 fusion.22
  616.7 163.7 %all-gather.14.cloned.1.call-done = bf16[2048,4,768]{2,0,1:T(8,128)(2,1)} async-done(((bf16[256,4,768]{2,0,1:T(8,128)(2,1)}), bf16[2048,4,768]{2,0,1:T(8,128)(2,1)}) %all-gather.14.cloned.1.call-update) | async-done | bytes 12582928 | tf_op jit(solution)/shard_map/all_gather | solution.py:175
  780.5 11.3 multiply_convert_fusion.2
  791.7 7.0 fusion.72
  798.8 14.2 fusion.9
  813.0 1.2 concatenate.45
  814.2 2.6 gather_fusion.6
  816.8 3.0 reshape.497
  819.8 2.6 gather_fusion.5
  822.4 3.1 reshape.493
  825.6 16.2 multiply_reduce_fusion.2
  842.6 1.0 copy.188
  843.7 1.0 copy.186
  844.8 3.5 gather_fusion.7
  848.8 1.9 fusion.12
  850.8 1.4 multiply_reduce_fusion.8
  852.3 1.1 multiply_subtract_fusion.1
  853.4 0.9 copy-done.7
  854.3 1.9 fusion.24
  856.5 1.5 log_add_fusion
  858.0 2.8 convolution_convert_fusion
  860.7 1.9 copy.189
  862.7 2.1 multiply_reduce_fusion
  869.0 1.0 copy-done.3
  870.0 4.1 fusion.65
  874.2 1.1 copy-done.15
  875.3 11.6 convolution_bitcast_fusion.1
  887.7 0.9 copy.209
  888.6 20.1 convolution_bitcast_fusion
  908.8 1.3 fusion.75
  910.2 3.8 multiply_reduce_fusion.9
  914.0 1.3 fusion.74
  915.3 57.8 %copy.193 = f32[768,4,4096]{2,1,0:T(4,128)} copy(f32[768,4,4096]{0,2,1:T(8,128)} %convolution_bitcast_fusion) | data formatting | bytes 100663296 | tf_op jit(solution)/shard_map/ecd,ecf->def/transpose | solution.py:321
  973.1 2123.0 %all-reduce.18 = (bf16[768]{0:T(1024)(128)(2,1)S(1)}, bf16[768]{0:T(1024)(128)(2,1)S(1)}, bf16[768,4,4096]{2,1,0:T(4,128)(2,1)}) all-reduce(f32[768]{0:T(1024)S(1)} %get-tuple-element.90, f32[768]{0:T(1024)S(1)} %copy-done.78, f32[768,4,4096]{2,1,0:T(4,128)} %copy.193), channel_id=2, replica_groups=mesh['rep'=4,'shard'=8] {'shard'}, use_global_device_ids=true, to_apply=%region_30.33.clone | all-reduce | flops 12584448 | bytes 75506688
  3096.1 6.2 dynamic-slice_convert_fusion
  3102.3 1.6 convert_element_type.156
  3103.9 2.0 convert_element_type.154
  3105.9 3.2 convert_element_type.168
  3110.3 1.1 multiply_subtract_fusion
  3112.2 0.9 copy.208
  3114.0 8.9 all-reduce.12
  3125.7 88.7 %all-reduce.17.cloned.1.call-done = (bf16[256,4,768]{0,2,1:T(8,128)(2,1)}, bf16[96,2304]{1,0:T(8,128)(2,1)}, bf16[96,768]{1,0:T(8,128)(2,1)}, bf16[96,4,4096]{2,1,0:T(4,128)(2,1)}) async-done(((bf16[256,4,768]{0,2,1:T(8,128)(2,1)}, bf16[96,2304]{1,0:T(8,128)(2,1)}, bf16[96,768]{1,0:T(8,128)(2,1)}, bf16[96,4,4096]{2,1,0:T(4,128)(2,1)}), (bf16[256,4,768]{0,2,1:T(8,128)(2,1)}, bf16[96,2304]{1,0:T(8,128)(2,1)}, ...) | async-done | bytes 5308432 | tf_op jit(solution)/shard_map/psum | solution.py:352
  3214.4 1.6 convert_element_type.157
  3216.0 2.0 convert_element_type.155
  3218.0 4.0 copy.194
  3222.0 3.6 convert_element_type.167
  (349 shorter events, 34.0 us)
Async XLA Ops:
  7.2 112.3 %all-gather.8.cloned.1.call-start = ((), (), s32[]{:S(2)}) async-start(), calls=%async_computation.6 | async-start | bytes 3981312 | tf_op jit(solution)/shard_map/all_gather | solution.py:109
  7.9 119.2 %all-gather.10.cloned.1.call-start = ((), (), s32[]{:S(2)}) async-start(), calls=%async_computation.7 | async-start | bytes 1327104 | tf_op jit(solution)/shard_map/all_gather | solution.py:110
  8.7 593.3 %all-gather.12.cloned.1.call-start = ((), (), s32[]{:S(2)}) async-start(), calls=%async_computation.8 | async-start | bytes 28311552 | tf_op jit(solution)/shard_map/all_gather | solution.py:163
  14.0 2.8 copy-start.92
  14.0 26.3 copy-start.81
  14.0 27.0 copy-start.89
  14.1 28.2 copy-start.94
  14.1 28.5 copy-start.95
  14.1 46.5 %copy-start.90 = (bf16[96,4]{0,1:T(4,128)(2,1)S(1)}, bf16[96,4]{0,1:T(4,128)(2,1)}, u32[]{:S(2)}) copy-start(bf16[96,4]{0,1:T(4,128)(2,1)} %param.30) | copy-start | bytes 2308
  14.1 65.4 %copy-start.88 = (bf16[96,8]{0,1:T(8,128)(2,1)S(1)}, bf16[96,8]{0,1:T(8,128)(2,1)}, u32[]{:S(2)}) copy-start(bf16[96,8]{0,1:T(8,128)(2,1)} %param.29) | copy-start | bytes 4612
  14.1 91.6 %copy-start.56 = (s32[256,2]{0,1:T(2,128)S(1)}, s32[256,2]{0,1:T(2,128)}, u32[]{:S(2)}) copy-start(s32[256,2]{0,1:T(2,128)} %param.22) | copy-start | bytes 6148
  14.1 766.3 %all-gather.14.cloned.1.call-start = ((), (), s32[]{:S(2)}) async-start(), calls=%async_computation.9 | async-start | bytes 14155776 | tf_op jit(solution)/shard_map/all_gather | solution.py:175
  16.8 3085.5 %reduce-scatter.15.cloned.1.call-start = ((), (), s32[]{:S(2)}) async-start(), calls=%async_computation.11 | async-start | bytes 2654208 | tf_op jit(solution)/shard_map/reduce_scatter | solution.py:313
  60.6 69.2 %copy-start.50 = (f32[768]{0:T(1024)}, f32[768]{0:T(1024)S(1)}, u32[]{:S(2)}) copy-start(f32[768]{0:T(1024)S(1)} %convert_element_type.138) | copy-start | bytes 9220
  106.0 5.7 copy-start.36
  106.3 8.2 copy-start.4
  115.2 3.6 copy-start.86
  117.3 663.1 %copy-start.42 = (pred[4,64]{1,0:T(4,128)(4,1)}, pred[4,64]{1,0:T(4,128)(4,1)S(1)}, u32[]{:S(2)}) copy-start(pred[4,64]{1,0:T(4,128)(4,1)S(1)} %compare_and_fusion.2) | copy-start | bytes 772
  117.9 5.2 copy-start.48
  118.7 4.5 copy-start.32
  118.7 4.5 copy-start.34
  127.0 3.6 copy-start.20
  127.1 3.6 copy-start.83
  131.6 4.2 copy-start.37
  131.6 4.3 copy-start.57
  135.6 3.6 copy-start.80
  137.7 5.2 copy-start.63
  137.8 5.1 copy-start.40
  137.8 5.1 copy-start.59
  137.9 5.0 copy-start.65
  142.9 473.8 %copy-start.5 = (bf16[256,768]{1,0:T(8,128)(2,1)}, bf16[256,768]{1,0:T(8,128)(2,1)S(1)}, u32[]{:S(2)}) copy-start(bf16[256,768]{1,0:T(8,128)(2,1)S(1)} %gather_fusion.1) | copy-start | bytes 1179652
  143.1 637.3 %copy-start.54 = (f32[4,64]{1,0:T(4,128)}, f32[4,64]{1,0:T(4,128)S(1)}, u32[]{:S(2)}) copy-start(f32[4,64]{1,0:T(4,128)S(1)} %fusion.33) | copy-start | bytes 3076
  791.7 7.0 copy-start.13
  822.4 3.2 copy-start.12
  822.4 3.2 copy-start.30
  822.4 3.2 copy-start.31
  822.4 3.2 copy-start.39
  822.4 3.2 copy-start.70
  825.6 16.3 copy-start.69
  825.6 18.1 copy-start.41
  825.6 18.1 copy-start.60
  825.6 18.1 copy-start.66
  825.6 19.1 copy-start.85
  825.6 19.1 copy-start.93
  844.8 3.8 copy-start.58
  844.8 3.9 copy-start.68
  844.8 3.9 copy-start.73
  844.8 3.9 copy-start.64
  844.8 3.9 copy-start.74
  844.8 3.9 copy-start.75
  848.3 2.4 copy-start.10
  848.7 3.5 copy-start.44
  848.8 3.5 copy-start.61
  856.2 6.5 copy-start.1
  856.2 2247.8 %reduce-scatter.13.cloned.1.call-start = ((), (), s32[]{:S(2)}) async-start(), calls=%async_computation.10 | async-start | bytes 7962624 | tf_op jit(solution)/shard_map/reduce_scatter | solution.py:312
  874.1 2231.8 %reduce-scatter.17.cloned.1.call-start = ((), (), s32[]{:S(2)}) async-start(), calls=%async_computation.12 | async-start | bytes 28311552 | tf_op jit(solution)/shard_map/reduce_scatter | solution.py:327
  886.9 2224.5 %reduce-scatter.23.cloned.1.call-start = ((), (), s32[]{:S(2)}) async-start(), calls=%async_computation.15 | async-start | bytes 442368
  888.6 20.2 copy-start.62
  908.7 2203.5 %reduce-scatter.21.cloned.1.call-start = ((), (), s32[]{:S(2)}) async-start(), calls=%async_computation.14 | async-start | bytes 442368
  910.1 3.9 copy-start.45
  910.1 2203.0 %reduce-scatter.19.cloned.1.call-start = ((), (), s32[]{:S(2)}) async-start(), calls=%async_computation.13 | async-start | bytes 442368
  915.3 57.8 %copy-start.78 = (f32[768]{0:T(1024)S(1)}, f32[768]{0:T(1024)}, u32[]{:S(2)}) copy-start(f32[768]{0:T(1024)} %get-tuple-element.88) | copy-start | bytes 9220
  973.1 2241.3 %all-reduce.17.cloned.1.call-start = ((), (), s32[]{:S(2)}) async-start(), calls=%async_computation.16 | async-start | bytes 10616832 | tf_op jit(solution)/shard_map/psum | solution.py:352
  3218.0 4.0 copy-start.16
  (43 other events, 60.4 us)
Sparse Core Ops, SparseCore 0:
  10.2 68.3 all-gather.7
  80.8 39.7 all-gather.9
  122.8 479.1 all-gather.11
  604.0 176.3 all-gather.13
  856.3 67.3 reduce-scatter.14
  927.2 230.7 reduce-scatter.12
  1162.3 803.8 reduce-scatter.16
  1969.8 133.9 reduce-scatter.22
  2107.4 114.8 reduce-scatter.20
  2225.8 103.2 reduce-scatter.18
  3109.3 105.0 all-reduce.16
where the time goes:
time: 3240 us; the launch traced here: 3230 us
  blocking collectives  2220 us (69%)
  waiting for transfers between devices  713 us (22%)
  local copies, waits for them, and re-layouts  129 us (4%)
  matrix products  109 us (3%)
  other arithmetic  47.4 us (1%)
    unnamed x2, blocking collectives  2140 us
    all_gather x1, waiting for transfers between devices, local(): lax.all_gather(expert_in, 'shard', axis=0, tiled=True)  459 us
    all_gather x1, waiting for transfers between devices, local(): lax.all_gather(expert_out, 'shard', axis=0, tiled=True)  164 us
    psum x1, waiting for transfers between devices, local(): lax.psum(out_share.astype(jnp.bfloat16), 'rep').astype(jnp.float32)  88.7 us
  transfers between devices with their start and end apart: 11, of which 3 were waited for; matrix products, arithmetic and copies ran while one was open for 6% of the time, Pallas kernels for 0%

commit v1 on v0

v1 whole, which is shorter than its diff:
```python
import math

import jax
import jax.numpy as jnp
import numpy as np
from jax import lax
from jax.experimental import pallas as pl
from jax.experimental.pallas import tpu as pltpu
from jax.sharding import PartitionSpec as P

H = 12
HD = 64
FF = 2048
E_FFN = 4
NC = 2
NE = 8
CAP = 64
D = 768
T = 256
GROUP = 8
ROWS = D // GROUP
HALF = ROWS // 2
WIDE = 2 * D
QUARTER = FF // 4

EPSILON = 1e-06
BF = jnp.bfloat16
F32 = jnp.float32
I32 = jnp.int32
AXES = ("rep", "shard")
VMEM_LIMIT = 56 << 20


def nn(a, b):
    return lax.dot_general(a, b, (((1,), (0,)), ((), ())), preferred_element_type=F32)


def nt(a, b):
    return lax.dot_general(a, b, (((1,), (1,)), ((), ())), preferred_element_type=F32)


def tn(a, b):
    return lax.dot_general(a, b, (((0,), (0,)), ((), ())), preferred_element_type=F32)


def exact(a, b, dims):
    return lax.dot_general(
        a, b, (dims, ((), ())), precision=lax.Precision.HIGHEST, preferred_element_type=F32
    )


def iota(shape, dim):
    return lax.broadcasted_iota(I32, shape, dim)


def split(v):
    high = v.astype(BF)
    return high, (v - high.astype(F32)).astype(BF)


def tables():
    half = HD // 2
    position = np.arange(T, dtype=np.float32)
    frequency = np.exp(
        np.arange(half, dtype=np.float32) * np.float32(-2.0 * math.log(10000.0) / HD)
    ).astype(np.float32)
    angle = (position[:, None] * frequency[None, :]).astype(np.float32)
    cosine, sine = np.cos(angle), np.sin(angle)
    return (
        np.concatenate([cosine] * 4, axis=1).astype(np.float32),
        np.concatenate([-sine, sine] * 2, axis=1).astype(np.float32),
    )


def swapped(tile):
    lane = iota(tile.shape, 1) % HD
    return jnp.where(lane < HD // 2, pltpu.roll(tile, 96, 1), pltpu.roll(tile, 32, 1))


def call(body, out_shape, in_specs, scratch=(), flops=0, moved=0):
    return pl.pallas_call(
        body,
        out_shape=out_shape,
        in_specs=in_specs,
        out_specs=jax.tree.map(lambda _: pl.BlockSpec(memory_space=pltpu.VMEM), out_shape),
        scratch_shapes=list(scratch),
        compiler_params=pltpu.CompilerParams(vmem_limit_bytes=VMEM_LIMIT),
        cost_estimate=pl.CostEstimate(flops=flops, bytes_accessed=moved, transcendentals=0),
    )


SMEM = pl.BlockSpec(memory_space=pltpu.SMEM)
VM = pl.BlockSpec(memory_space=pltpu.VMEM)
ANY = pl.BlockSpec(memory_space=pl.ANY)


def shape(*dims, dtype=BF):
    return jax.ShapeDtypeStruct(dims, dtype)


def start_weights(pos, pieces, target, sems):
    x, c, z, y = (pos[i] for i in range(4))
    copies = []
    for p in range(4):
        column = pl.multiple_of((x ^ (p >> 1)) * WIDE, 128)
        for cr in range(2):
            for kz in range(4):
                row = ((z ^ kz) * 2 + (y ^ (p & 1))) * ROWS + (c ^ cr) * HALF
                copies.append(
                    pltpu.make_async_copy(
                        pieces[2 * p + cr].at[pl.ds(kz * HALF, HALF), :],
                        target.at[pl.ds(pl.multiple_of(row, 16), HALF), pl.ds(column, WIDE)],
                        sems.at[len(copies)],
                    )
                )
    for copy in copies:
        copy.start()
    return copies


def route_body(pos, routes, order, grad, prev, g0, g1, g2, g3, disp_out):
    here = 2 * pos[0] + pos[3]
    row, col = iota((T, T), 0), iota((T, T), 1)
    lane = iota((T, 16), 1)
    claims = jnp.where(order[...] == row, 1.0, 0.0).astype(BF)
    r = routes[...]
    chosen = ((r[:, 0:1] == lane) | (r[:, 1:2] == lane)) & (lane < E_FFN)
    ranked = tn(claims, jnp.where(chosen, 1.0, 0.0).astype(BF))
    before = nn(jnp.where(col < row, 1.0, 0.0).astype(BF), ranked.astype(BF))
    place = nn(claims, before.astype(BF))
    kept = chosen & (place < CAP)
    dispatch = jnp.zeros((T, T), F32)
    colf = col.astype(F32)
    for p in range(4):
        mine = kept & (lane == (here ^ p))
        target = jnp.sum(jnp.where(mine, place + (p * CAP + 1.0), 0.0), axis=1, keepdims=True)
        dispatch = dispatch + jnp.where(colf == target - 1.0, 1.0, 0.0)
    dispatch = dispatch.astype(BF)
    disp_out[...] = dispatch
    slots = tn(dispatch, grad[...].astype(BF)).astype(BF)
    extra = tn(dispatch, prev[...]).astype(BF)
    for p, out in enumerate((g0, g1, g2, g3)):
        out[:, :D] = slots[p * CAP : (p + 1) * CAP]
        out[:, D:] = extra[p * CAP : (p + 1) * CAP]


def attend_body(
    pos, stream, small, seg, cos, sin, disp, w0, w1, w2, w3, w4, w5, w6, w7,
    normed_out, q_out, k_out, v_out, probs_out, mixed_out, hidden_out, routed_out,
    x0, x1, x2, x3, weights, sems,
):
    copies = start_weights(pos, (w0, w1, w2, w3, w4, w5, w6, w7), weights, sems)
    s = stream[...]
    r1 = lax.rsqrt(jnp.mean(s * s, axis=1, keepdims=True) + EPSILON)
    normed = (s * r1 * small[14:15, :].astype(F32)).astype(BF)
    normed_out[...] = normed
    row, col = iota((T, T), 0), iota((T, T), 1)
    segf = seg[...].astype(F32)
    segcol = jnp.sum(jnp.where(row == col, segf, 0.0), axis=1, keepdims=True)
    allowed = (segcol == segf) & (col <= row)
    cosine, sine = cos[...], sin[...]
    for copy in copies:
        copy.wait()
    for n in range(9):
        part = nn(normed, weights[:, n * 256 : (n + 1) * 256])
        out, base = (q_out, k_out, v_out)[n // 3], (n % 3) * 256
        for t in range(2):
            tile = part[:, t * 128 : (t + 1) * 128]
            if n < 6:
                tile = tile * cosine + swapped(tile) * sine
            out[:, base + t * 128 : base + (t + 1) * 128] = tile.astype(BF)
    first = iota((T, 128), 1) < HD
    for j in range(H // 2):
        cols = slice(j * 128, (j + 1) * 128)
        q2, k2, v2 = q_out[:, cols], k_out[:, cols], v_out[:, cols]
        halves = []
        for hh in range(2):
            mask = first if hh == 0 else ~first
            qm = jnp.where(mask, q2.astype(F32), 0.0).astype(BF)
            scores = jnp.where(allowed, nt(qm, k2) * (1.0 / math.sqrt(HD)), -1e30)
            raised = jnp.exp(scores - jnp.max(scores, axis=1, keepdims=True))
            probs = (raised / jnp.sum(raised, axis=1, keepdims=True)).astype(BF)
            probs_out[2 * j + hh] = probs
            halves.append(nn(probs, v2))
        mixed_out[:, cols] = jnp.where(first, halves[0], halves[1]).astype(BF)
    hidden = s + nn(mixed_out[...], weights[:, 3 * D :])
    hidden_out[...] = hidden
    r2 = lax.rsqrt(jnp.mean(hidden * hidden, axis=1, keepdims=True) + EPSILON)
    routed = (hidden * r2 * small[15:16, :].astype(F32)).astype(BF)
    routed_out[...] = routed
    slots = tn(disp[...], routed).astype(BF)
    for p, out in enumerate((x0, x1, x2, x3)):
        out[...] = slots[p * CAP : (p + 1) * CAP]


def column(v, lane, index):
    return jnp.sum(jnp.where(lane == index, v, 0.0), axis=1, keepdims=True)


def chance(logits, lane):
    masked = jnp.where(lane < NE, logits, -1e30)
    raised = jnp.where(lane < NE, jnp.exp(masked - jnp.max(masked, axis=1, keepdims=True)), 0.0)
    return raised / jnp.sum(raised, axis=1, keepdims=True)


def router_body(hidden, routed, small, prev, routes, grad, base_out, aux_out):
    lane = iota((T, 16), 1)
    rin = routed[...].astype(F32)
    g = grad[...]
    logits = nt(routed[...], small[...])
    chances = chance(logits + prev[...], lane)
    r = routes[...]
    chosen = (r[:, 0:1] == lane) | (r[:, 1:2] == lane)
    combine = jnp.where(chosen, chances, 0.0)
    copy_weight = column(combine, lane, E_FFN + 1)
    copy_grad = jnp.sum(g * rin, axis=1, keepdims=True)
    base = hidden[...] + copy_weight * rin
    others = jnp.where(lane == E_FFN + 1, copy_grad, 0.0)
    mixing_grad = jnp.zeros((T, 16), F32)
    factor = copy_weight
    for n in range(NC):
        l0, l1 = column(logits, lane, 8 + 2 * n), column(logits, lane, 9 + 2 * n)
        a0, a1 = 1.0 / (1.0 + jnp.exp(l1 - l0)), 1.0 / (1.0 + jnp.exp(l0 - l1))
        vector = small[12 + n : 13 + n, :].astype(F32)
        weight = column(combine, lane, E_FFN + 2 + n)
        base = base + weight * (a0 * rin + a1 * vector)
        vector_dot = jnp.sum(g * vector, axis=1, keepdims=True)
        others = others + jnp.where(
            lane == E_FFN + 2 + n, a0 * copy_grad + a1 * vector_dot, 0.0
        )
        d0, d1 = weight * copy_grad, weight * vector_dot
        total = a0 * d0 + a1 * d1
        mixing_grad = mixing_grad + jnp.where(lane == 8 + 2 * n, a0 * (d0 - total), 0.0)
        mixing_grad = mixing_grad + jnp.where(lane == 9 + 2 * n, a1 * (d1 - total), 0.0)
        mixing_grad = mixing_grad + jnp.where(lane == 12 + n, a1 * weight, 0.0)
        factor = factor + a0 * weight
    base_out[...] = base
    aux_out[:, 0:16] = chances
    aux_out[:, 16:32] = combine
    aux_out[:, 32:48] = jnp.where(chosen, others, 0.0)
    aux_out[:, 48:64] = mixing_grad
    aux_out[:, 64:128] = jnp.broadcast_to(factor, (T, 64))


def expert_body(
    pos, x0, x1, x2, x3, g0, g1, g2, g3, v0, v1, v2, v3, e0, e1, e2, e3,
    send_out, keep_out, act_out, grad_out, win_out, wout_out,
):
    z, y = pos[2], pos[3]
    for kz, piece in enumerate((v0, v1, v2, v3)):
        for yr in range(2):
            row = pl.multiple_of(((z ^ kz) * 2 + (y ^ yr)) * ROWS, 16)
            win_out[pl.ds(row, ROWS), :] = piece[yr * ROWS : (yr + 1) * ROWS, :]
    wout_out[:256] = e0[...] + e1[...]
    wout_out[256:] = e2[...] + e3[...]
    win, wout = win_out[...], wout_out[...]
    ones = jnp.ones((16, QUARTER), F32)
    for b, (xs, gs) in enumerate(((x0, g0), (x1, g1), (x2, g2), (x3, g3))):
        rows = slice(b * 256, (b + 1) * 256)
        gate_up = nn(xs[...], win)
        a, u = gate_up[:, :QUARTER], gate_up[:, QUARTER:]
        sigma = 1.0 / (1.0 + jnp.exp(-a))
        swish = a * sigma
        activated = (swish * u).astype(BF)
        act_out[rows, :] = activated
        back = nt(gs[:, :D], wout)
        dots = exact(ones, activated.astype(F32) * back, ((1,), (1,)))[0:1]
        gate_grad = back * u * sigma * (1.0 + a * (1.0 - sigma))
        both = jnp.concatenate([gate_grad.astype(BF), (back * swish).astype(BF)], axis=1)
        grad_out[rows, :] = both
        slot_grad = nt(both, win)
        at = (b % 2) * 272
        if b < 2:
            keep_out[at : at + 256, :] = slot_grad
            keep_out[at + 256 : at + 272, :] = jnp.zeros((16, D), F32)
            keep_out[at + 256 : at + 257, 0:256] = dots
        else:
            high, low = split(dots)
            send_out[at : at + 256, :] = slot_grad.astype(BF)
            send_out[at + 256 : at + 272, :] = jnp.zeros((16, D), BF)
            send_out[at + 256 : at + 258, 0:256] = jnp.concatenate([high, low], axis=0)


def fold_body(keep, got, send_out, keep_out):
    total = keep[...] + got[...].astype(F32)
    dots = [keep[n * 272 + 256 : n * 272 + 257, 0:256]
            + got[n * 272 + 256 : n * 272 + 257, 0:256].astype(F32)
            + got[n * 272 + 257 : n * 272 + 258, 0:256].astype(F32) for n in range(2)]
    keep_out[0:256, :] = total[0:256]
    keep_out[256:272, :] = jnp.zeros((16, D), F32)
    keep_out[256:257, 0:256] = dots[0]
    high, low = split(dots[1])
    send_out[0:256, :] = total[272:528].astype(BF)
    send_out[256:272, :] = jnp.zeros((16, D), BF)
    send_out[256:258, 0:256] = jnp.concatenate([high, low], axis=0)


def spread_body(keep, got, r0, r1, r2, r3):
    total = (keep[0:256, :] + got[0:256, :].astype(F32)).astype(BF)
    dots = (
        keep[256:257, 0:256] + got[256:257, 0:256].astype(F32) + got[257:258, 0:256].astype(F32)
    )
    high, low = split(dots)
    for p, out in enumerate((r0, r1, r2, r3)):
        out[0:CAP, :] = total[p * CAP : (p + 1) * CAP]
        out[CAP : CAP + 16, :] = jnp.zeros((16, D), BF)
        out[CAP : CAP + 2, 0:256] = jnp.concatenate([high, low], axis=0)


def slots_out_body(act, wout, send_out, keep_out):
    for b in range(4):
        part = nn(act[b * 256 : (b + 1) * 256, :], wout[...]).astype(BF)
        out = (keep_out, send_out)[b // 2]
        out[(b % 2) * 256 : (b % 2 + 1) * 256, :] = part


def weight_grad_body(
    pos, x0, x1, x2, x3, g0, g1, g2, g3, act, grad, small,
    d0, d1, d2, d3, o0, o1, scaled, whole,
):
    x, z, y = pos[0], pos[2], pos[3]
    lane = iota((256, 16), 1)
    expert = 2 * x + y
    total = jnp.zeros((QUARTER, D), F32)
    xs = jnp.concatenate([v[...] for v in (x0, x1, x2, x3)], axis=0)
    for b, (xv, gs) in enumerate(((x0, g0), (x1, g1), (x2, g2), (x3, g3))):
        rows = slice(b * 256, (b + 1) * 256)
        prev = gs[:, D : D + 16].astype(F32) + gs[:, D + 16 : D + 32].astype(F32)
        chances = chance(nt(xv[...], small[...]) + jnp.where(lane < NE, prev, 0.0), lane)
        weight = column(chances, lane, expert)
        scaled[rows, :] = (grad[rows, :].astype(F32) * weight).astype(BF)
        total = total + tn(act[rows, :], (gs[:, :D].astype(F32) * weight).astype(BF))
    o0[...] = total[:256].astype(BF)
    o1[...] = total[256:].astype(BF)
    for n in range(4):
        cols = slice(n * 256, (n + 1) * 256)
        whole[:, cols] = tn(xs, scaled[:, cols]).astype(BF)
    for kz, out in enumerate((d0, d1, d2, d3)):
        for yr in range(2):
            row = pl.multiple_of(((z ^ kz) * 2 + (y ^ yr)) * ROWS, 16)
            out[yr * ROWS : (yr + 1) * ROWS, :] = whole[pl.ds(row, ROWS), :]


def back_body(
    pos, r0, r1, r2, r3, disp, hidden_in, routed, aux, grad, small, stream, normed, q, k, v,
    probs, mixed, cos, sin, w0, w1, w2, w3, w4, w5, w6, w7,
    stream_out, logits_out, small_out, send_out, keep_out, weights, sems, pgrad, whole,
):
    copies = start_weights(pos, (w0, w1, w2, w3, w4, w5, w6, w7), weights, sems)
    x, c, z, y = (pos[i] for i in range(4))
    here = 2 * x + y
    lane = iota((T, 16), 1)
    block = iota((T, T), 1) // CAP
    block_row = iota((1, T), 1) // CAP
    dispf = disp[...].astype(F32)
    g, hidden, rin = grad[...], hidden_in[...], routed[...].astype(F32)
    chances, combine = aux[:, 0:16], aux[:, 16:32]
    dots = jnp.zeros((1, T), F32)
    weight = jnp.zeros((T, T), F32)
    chance_grad = aux[:, 32:48]
    for p, r in enumerate((r0, r1, r2, r3)):
        part = r[CAP : CAP + 1, 0:T].astype(F32) + r[CAP + 1 : CAP + 2, 0:T].astype(F32)
        dots = jnp.where(block_row == p, part, dots)
        weight = jnp.where(block == p, column(combine, lane, here ^ p), weight)
    picked = dispf * dots
    for p in range(4):
        each = jnp.sum(jnp.where(block == p, picked, 0.0), axis=1, keepdims=True)
        chance_grad = chance_grad + jnp.where(lane == (here ^ p), each, 0.0)
    logit_grad = chances * (chance_grad - jnp.sum(chances * chance_grad, axis=1, keepdims=True))
    logits_out[...] = logit_grad[:, 0:NE]
    extra = aux[:, 48:64]
    mix_grad = jnp.where((lane >= 8) & (lane < 12), extra, 0.0)
    all_grad = logit_grad + mix_grad
    returned = jnp.concatenate([r[0:CAP, :] for r in (r0, r1, r2, r3)], axis=0)
    high, low = split(dispf * weight)
    smallf = small[...].astype(F32)
    routed_grad = (
        aux[:, 64:65] * g + nn(high, returned) + nn(low, returned)
        + exact(all_grad, smallf, ((1,), (0,)))
    )
    r2n = lax.rsqrt(jnp.mean(hidden * hidden, axis=1, keepdims=True) + EPSILON)
    scaled = routed_grad * smallf[15:16, :]
    hidden_grad = (
        g + r2n * scaled
        - hidden * (r2n * r2n * r2n) * jnp.mean(scaled * hidden, axis=1, keepdims=True)
    )
    attn_grad = hidden_grad.astype(BF)
    small_out[...] = exact(all_grad, rin, ((0,), (0,)))
    vector_grad = exact(jnp.where(lane >= 12, extra, 0.0), g, ((0,), (0,)))
    small_out[12:14, :] = vector_grad[12:14, :]
    small_out[15:16, :] = jnp.sum(routed_grad * hidden * r2n, axis=0, keepdims=True)
    for copy in copies:
        copy.wait()
    mixed_grad = nt(attn_grad, weights[:, 3 * D :]).astype(BF)
    whole[:, 3 * D :] = tn(mixed[...], attn_grad).astype(BF)
    first = iota((T, 128), 1) < HD
    cosine, sine = cos[...], sin[...]
    scale = 1.0 / math.sqrt(HD)
    for j in range(H // 2):
        cols = slice(j * 128, (j + 1) * 128)
        q2, k2, v2, do2 = q[:, cols], k[:, cols], v[:, cols], mixed_grad[:, cols]
        parts = []
        for hh in range(2):
            mask = first if hh == 0 else ~first
            do = jnp.where(mask, do2.astype(F32), 0.0).astype(BF)
            pb = probs[2 * j + hh]
            pf = pb.astype(F32)
            prob_grad = nt(do, v2)
            inner = jnp.sum(pf * prob_grad, axis=1, keepdims=True)
            score_grad = (pf * (prob_grad - inner)).astype(BF)
            parts.append((nn(score_grad, k2), tn(score_grad, q2), tn(pb, do2)))
        dq, dk, dv = (jnp.where(first, parts[0][n], parts[1][n]) for n in range(3))
        dq, dk = dq * scale, dk * scale
        pgrad[:, j * 128 : (j + 1) * 128] = (dq * cosine - swapped(dq) * sine).astype(BF)
        pgrad[:, D + j * 128 : D + (j + 1) * 128] = (dk * cosine - swapped(dk) * sine).astype(BF)
        pgrad[:, 2 * D + j * 128 : 2 * D + (j + 1) * 128] = dv.astype(BF)
    for n in range(9):
        cols = slice(n * 256, (n + 1) * 256)
        whole[:, cols] = tn(normed[...], pgrad[:, cols]).astype(BF)
    normed_grad = nt(pgrad[...], weights[:, : 3 * D])
    s = stream[...]
    r1n = lax.rsqrt(jnp.mean(s * s, axis=1, keepdims=True) + EPSILON)
    scaled = normed_grad * smallf[14:15, :]
    stream_out[...] = (
        hidden_grad + r1n * scaled
        - s * (r1n * r1n * r1n) * jnp.mean(scaled * s, axis=1, keepdims=True)
    )
    small_out[14:15, :] = jnp.sum(normed_grad * s * r1n, axis=0, keepdims=True)
    for p in range(4):
        at = pl.multiple_of((x ^ (p >> 1)) * WIDE, 128)
        for cr, out in enumerate((keep_out, send_out)):
            for kz in range(4):
                row = ((z ^ kz) * 2 + (y ^ (p & 1))) * ROWS + (c ^ cr) * HALF
                out[p, kz * HALF : (kz + 1) * HALF, :] = whole[
                    pl.ds(pl.multiple_of(row, 16), HALF), pl.ds(at, WIDE)
                ]


def result_body(pos, base, disp, aux, r0, r1, r2, r3, out):
    here = 2 * pos[0] + pos[3]
    lane = iota((T, 16), 1)
    block = iota((T, T), 1) // CAP
    combine = aux[:, 16:32]
    weight = jnp.zeros((T, T), F32)
    for p in range(4):
        weight = jnp.where(block == p, column(combine, lane, here ^ p), weight)
    high, low = split(disp[...].astype(F32) * weight)
    returned = jnp.concatenate([r[...] for r in (r0, r1, r2, r3)], axis=0)
    out[...] = (base[...] + nn(high, returned) + nn(low, returned)).astype(BF)


def place_body(pos, own, over, other, out):
    x, c, z, y = (pos[i] for i in range(4))
    for xr in range(2):
        for cr in range(2):
            for yr in range(2):
                for zr in range(2):
                    source = other if cr else (over if xr else own)
                    n = 2 * yr + zr + (4 * xr if cr else 0)
                    expert = 2 * (x ^ xr) + (y ^ yr)
                    quarter = 2 * ((z & 1) ^ zr) + (c ^ cr)
                    for half in range(2):
                        for o in range(2):
                            at = half * FF + quarter * QUARTER + ((y ^ yr) ^ o) * 256
                            m = 2 * half + o
                            out[expert, :, pl.ds(pl.multiple_of(at, 256), 256)] = source[
                                n, :, m * 256 : (m + 1) * 256
                            ]


def plan(mesh):
    reps, shards = mesh.shape["rep"], mesh.shape["shard"]
    spread = shards // GROUP
    assert reps == E_FFN and shards % GROUP == 0
    lows = [[hi * spread + lo for lo in range(spread)] for hi in range(GROUP)]

    def flat(rep, hi, lo):
        return rep * shards + hi * spread + lo

    def hop(value, rmask, hmask):
        pairs = [
            (flat(r, h, w), flat(r ^ rmask, h ^ hmask, w))
            for r in range(reps) for h in range(GROUP) for w in range(spread)
        ]
        return lax.ppermute(value, AXES, pairs)

    def owners(ky, up, back=False):
        pairs = []
        for r in range(reps):
            for zl in range(2):
                for y in range(2):
                    for w in range(spread):
                        source = flat(r, 2 * (2 * zl + (r & 1)) + (y ^ ky), w)
                        target = flat(r, 2 * (zl + 2 * up) + y, w)
                        pairs.append((target, source) if back else (source, target))
        return pairs

    def pick(bit, pair):
        return (jnp.where(bit == 0, pair[0], pair[1]), jnp.where(bit == 0, pair[1], pair[0]))

    XY = ((0, 0), (0, 1), (2, 0), (2, 1))
    cos_table, sin_table = tables()

    def local(
        stream, prev_logits, segments, routes, claim_order, out_cotangent,
        first_gain, attend_weight, output_weight, second_gain, router_weight,
        constant_mix, constant_vector, expert_in, expert_out,
    ):
        rep, shard = lax.axis_index("rep"), lax.axis_index("shard")
        high = shard // spread
        x, c, z, y = rep // 2, rep % 2, high // 2, high % 2
        pos = jnp.stack([x, c, z, y]).astype(I32)
        own_rows = first_gain.shape[0]

        small = jnp.concatenate(
            [router_weight, constant_mix, constant_vector, first_gain[:, None], second_gain[:, None]],
            axis=1,
        )
        small = lax.all_gather(small, "shard", axis=0, tiled=True).T

        if spread > 1:
            attend_weight, output_weight, expert_in, expert_out = (
                lax.all_gather(v, "shard", axis_index_groups=lows, axis=0, tiled=True)
                for v in (attend_weight, output_weight, expert_in, expert_out)
            )

        both = jnp.concatenate([attend_weight, output_weight], axis=1)
        mine = lax.dynamic_slice(both, (c * HALF, x * WIDE), (HALF, WIDE))
        column_part = jnp.concatenate([mine] + [hop(mine, 0, 2 * kz) for kz in (1, 2, 3)], axis=0)
        plane = [column_part] + [hop(column_part, *XY[p]) for p in (1, 2, 3)]
        pieces = []
        for p in range(4):
            pieces += [plane[p], hop(plane[p], 1, 0)]

        prev16 = jnp.concatenate([prev_logits, jnp.zeros((T, 16 - NE), F32)], axis=1)
        prev_high, prev_low = split(prev16)
        prevx = jnp.concatenate([prev_high, prev_low, jnp.zeros((T, 96), BF)], axis=1)
        *g_parts, disp = call(
            route_body,
            (shape(CAP, D + 128),) * 4 + (shape(T, T),),
            [SMEM] + [VM] * 4,
            flops=2 * T * T * 900,
            moved=2 << 20,
        )(pos, routes, claim_order, out_cotangent, prevx)

        def dispatch(parts):
            first = jnp.concatenate(
                [parts[0]] + [hop(parts[p], *XY[p]) for p in (1, 2, 3)], axis=0
            )
            second = hop(first, 0, 2)
            return first, second, hop(first, 1, 0), hop(second, 1, 0)

        g_slots = dispatch(g_parts)

        def columns(yr, zr):
            yd = y ^ yr
            quarter = 2 * ((z & 1) ^ zr) + c
            return jnp.concatenate(
                [
                    lax.dynamic_slice(
                        expert_in,
                        (0, 2 * x + yd, half * FF + quarter * QUARTER + (yd ^ o) * 256),
                        (ROWS, 1, 256),
                    )[:, 0]
                    for half in range(2) for o in range(2)
                ],
                axis=1,
            )

        across = hop(jnp.stack([columns(1, 0), columns(1, 1)]), 0, 1)
        joined = [jnp.concatenate([columns(0, zr), across[zr]], axis=0) for zr in range(2)]
        win_parts = [joined[0]] + [hop(joined[kz & 1], 0, 2 * kz) for kz in (1, 2, 3)]
        wout_parts = []
        for ky in range(2):
            rows = lax.dynamic_slice(
                expert_out, (0, 2 * x + (y ^ ky), 0), (expert_out.shape[0], 1, D)
            )[:, 0]
            for up in range(2):
                wout_parts.append(lax.ppermute(rows, AXES, owners(ky, up)))

        normed, q, k, v, probs, mixed, hidden, routed, *x_parts = call(
            attend_body,
            (shape(T, D),) * 4 + (shape(H, T, T), shape(T, D), shape(T, D, dtype=F32))
            + (shape(T, D),) + (shape(CAP, D),) * 4,
            [SMEM] + [VM] * 6 + [ANY] * 8,
            [pltpu.VMEM((D, 4 * D), BF), pltpu.SemaphoreType.DMA((32,))],
            flops=2 * T * D * 4 * D + 4 * H * T * T * 128,
            moved=10 << 20,
        )(pos, stream, small, segments, cos_table, sin_table, disp, *pieces)

        x_slots = dispatch(x_parts)

        base, aux = call(
            router_body,
            (shape(T, D, dtype=F32), shape(T, 128, dtype=F32)),
            [VM] * 6,
            flops=20 * T * D,
            moved=4 << 20,
        )(hidden, routed, small, prev16, routes, out_cotangent)

        send, keep, act, gate_up_grad, _, wout = call(
            expert_body,
            (shape(544, D), shape(544, D, dtype=F32), shape(1024, QUARTER),
             shape(1024, 2 * QUARTER), shape(D, 2 * QUARTER), shape(QUARTER, D)),
            [SMEM] + [VM] * 16,
            flops=2 * 1024 * D * 5 * QUARTER,
            moved=12 << 20,
        )(pos, *x_slots, *g_slots, *win_parts, *wout_parts)
        got = hop(send, 1, 0)
        send, keep = call(
            fold_body, (shape(272, D), shape(272, D, dtype=F32)), [VM] * 2, moved=4 << 20
        )(keep, got)
        got = hop(send, 0, 2)
        back_parts = call(spread_body, (shape(CAP + 16, D),) * 4, [VM] * 2, moved=2 << 20)(keep, got)
        back_parts = [back_parts[0]] + [hop(back_parts[p], *XY[p]) for p in (1, 2, 3)]

        out_send, out_keep = call(
            slots_out_body, (shape(512, D),) * 2, [VM] * 2, flops=2 * 1024 * QUARTER * D, moved=4 << 20
        )(act, wout)
        *win_grads, wout_grad0, wout_grad1 = call(
            weight_grad_body,
            (shape(2 * ROWS, 2 * QUARTER),) * 4 + (shape(256, D),) * 2,
            [SMEM] + [VM] * 11,
            [pltpu.VMEM((1024, 2 * QUARTER), BF), pltpu.VMEM((D, 2 * QUARTER), BF)],
            flops=2 * 1024 * D * 3 * QUARTER,
            moved=12 << 20,
        )(pos, *x_slots, *g_slots, act, gate_up_grad, small)

        stream_grad, logits_grad, small_grad, w_send, w_keep = call(
            back_body,
            (shape(T, D, dtype=F32), shape(T, NE, dtype=F32), shape(16, D, dtype=F32),
             shape(4, 4 * HALF, WIDE), shape(4, 4 * HALF, WIDE)),
            [SMEM] + [VM] * 19 + [ANY] * 8,
            [pltpu.VMEM((D, 4 * D), BF), pltpu.SemaphoreType.DMA((32,)),
             pltpu.VMEM((T, 3 * D), BF), pltpu.VMEM((D, 4 * D), BF)],
            flops=4 * T * D * 4 * D + 10 * H * T * T * 128,
            moved=24 << 20,
        )(pos, *back_parts, disp, hidden, routed, aux, out_cotangent, small, stream, normed,
          q, k, v, probs, mixed, cos_table, sin_table, *pieces)

        def add(a, b):
            return (a.astype(F32) + b.astype(F32)).astype(BF)

        out_sum = add(out_keep, hop(out_send, 1, 0))
        out_sum = add(out_sum[:256], hop(out_sum[256:], 0, 2))
        outs = [out_sum[p * CAP : (p + 1) * CAP] for p in range(4)]
        outs = [outs[0]] + [hop(outs[p], *XY[p]) for p in (1, 2, 3)]
        result = call(result_body, shape(T, D), [SMEM] + [VM] * 7, flops=4 * T * T * D, moved=3 << 20)(
            pos, base, disp, aux, *outs
        )

        arrived = [win_grads[0]] + [hop(win_grads[kz], 0, 2 * kz) for kz in (1, 2, 3)]
        sums = jnp.stack([add(arrived[0], arrived[2]), add(arrived[1], arrived[3])])
        other_y = hop(sums[:, ROWS:], 0, 1)
        own = jnp.concatenate([sums[:, :ROWS], other_y], axis=0)
        over = hop(own, 2, 0)
        other = hop(jnp.concatenate([own, over], axis=0), 1, 0)
        in_grad = call(place_body, shape(E_FFN, ROWS, 2 * FF), [SMEM] + [VM] * 3, moved=6 << 20)(
            pos, own, over, other
        )
        in_grad = in_grad.transpose(1, 0, 2).astype(F32)

        out_rows = []
        for ky, grad in enumerate((wout_grad0, wout_grad1)):
            a, b = (lax.ppermute(grad, AXES, owners(ky, up, True)) for up in range(2))
            out_rows.append(add(a, b))
        out_rows = jnp.stack(out_rows)
        out_rows = jnp.stack([out_rows, hop(out_rows, 2, 0)])
        out_rows = add(out_rows, hop(out_rows, 1, 0))
        by_x = pick(x, (out_rows[0], out_rows[1]))
        by_expert = [half for pair in by_x for half in pick(y, (pair[0], pair[1]))]
        out_grad = jnp.stack(by_expert, axis=1).astype(F32)

        total = add(w_keep, hop(w_send, 1, 0))
        parts = [total[0]] + [hop(total[p], *XY[p]) for p in (1, 2, 3)]
        total = add(add(parts[0], parts[1]), add(parts[2], parts[3]))
        parts = [total[kz * HALF : (kz + 1) * HALF] for kz in range(4)]
        parts = [parts[0]] + [hop(parts[kz], 0, 2 * kz) for kz in (1, 2, 3)]
        mine = add(add(parts[0], parts[1]), add(parts[2], parts[3]))
        wide = jnp.concatenate(pick(x, (mine, hop(mine, 2, 0))), axis=1)
        full = jnp.concatenate(pick(c, (wide, hop(wide, 1, 0))), axis=0).astype(F32)
        attend_grad, output_grad = full[:, : 3 * D], full[:, 3 * D :]

        if spread > 1:
            attend_grad, output_grad, in_grad, out_grad = (
                lax.psum_scatter(
                    v, "shard", scatter_dimension=0, axis_index_groups=lows, tiled=True
                )
                for v in (attend_grad, output_grad, in_grad, out_grad)
            )

        small_grad = lax.psum(small_grad, AXES)
        small_grad = lax.dynamic_slice(small_grad, (0, shard * own_rows), (16, own_rows))
        return (
            result,
            stream_grad,
            logits_grad,
            small_grad[14],
            attend_grad,
            output_grad,
            small_grad[15],
            small_grad[0:8].T,
            small_grad[8:12].T,
            small_grad[12:14].T,
            in_grad,
            out_grad,
        )

    return local


def solution(mesh):
    tokens = P(("rep", "shard"), None)
    weight = (P("shard"), P("shard", None), P("shard", None, None))
    return jax.shard_map(
        plan(mesh),
        mesh=mesh,
        in_specs=(tokens,) * 6
        + (weight[0], weight[1], weight[1], weight[0])
        + (weight[1],) * 3
        + (weight[2],) * 2,
        out_specs=(tokens,) * 3
        + (weight[0], weight[1], weight[1], weight[0])
        + (weight[1],) * 3
        + (weight[2],) * 2,
        check_vma=False,
    )
```

time: 3240 us -> 456 us (0.14)
  blocking collectives: 2220 us -> 92.1 us
  waiting for transfers between devices: 713 us -> 162 us
  matrix products: 109 us -> 0 us
  local copies, waits for them, and re-layouts: 129 us -> 43 us
  Pallas kernels: 0 us -> 70.1 us
  starting transfers between devices: 0.66 us -> 61.8 us
    unnamed x2 -> x0, blocking collectives: 2140 us -> none
    all_gather x4 -> x0, waiting for transfers between devices: 623 us -> none  [the longest x1 459 us: local(): lax.all_gather(expert_in, 'shard', axis=0, tiled=True)]
    ppermute x0 -> x61, waiting for transfers between devices: none -> 162 us  [the longest x53 162 us: hop(): return lax.ppermute(value, AXES, pairs)]
    dot_general x23 -> x0, matrix products: 107 us -> none  [the longest x1 20.1 us: local(): jnp.einsum('ecd,ecf->def', columns, gate_up_grad, preferred_element_type=...]
    psum x1 -> x0, waiting for transfers between devices: 88.7 us -> none  [local(): lax.psum(out_share.astype(jnp.bfloat16), 'rep').astype(jnp.float32)]
    pallas_call x0 -> x11, Pallas kernels: none -> 70.1 us  [the longest x1 18 us: local(): call(back_body, (shape(T, D, dtype=F32), shape(T, NE, dtype=F32), shape(1...]
    ppermute x0 -> x61, starting transfers between devices: none -> 61.8 us  [the longest x53 45.8 us: hop(): return lax.ppermute(value, AXES, pairs)]
    transpose x1 -> x3, local copies, waits for them, and re-layouts: 57.8 us -> 4.04 us  [the longest x1 1.36 us: local(): small_grad[0:8]]
  transfers between devices with their start and end apart: 11 -> 61, of which waited for: 3 -> 22; matrix products, arithmetic and copies ran while one was open for 6% -> 11% of each run, Pallas kernels for 0% -> 13%
where the time goes in v1:
time: 456 us; the launch traced here: 449 us
  waiting for transfers between devices  162 us (36%)
  blocking collectives  92.1 us (20%)
  Pallas kernels  70.1 us (15%)
  starting transfers between devices  61.8 us (14%)
  local copies, waits for them, and re-layouts  43 us (9%)
  other arithmetic  17.4 us (4%)
    ppermute x53, waiting for transfers between devices, hop(): return lax.ppermute(value, AXES, pairs)  162 us
    all_gather x1, blocking collectives, local(): small = lax.all_gather(small, 'shard', axis=0, tiled=True).T  53.3 us
    ppermute x53, starting transfers between devices, hop(): return lax.ppermute(value, AXES, pairs)  45.8 us
    psum x1, blocking collectives, local(): small_grad = lax.psum(small_grad, AXES)  38.9 us
    unnamed x114, local copies, waits for them, and re-layouts  27 us
    pallas_call x1, Pallas kernels, local(): call(back_body, (shape(T, D, dtype=F32), shape(T, NE, dtype=F32), shape(1...  18 us
    pallas_call x1, Pallas kernels, local(): call(expert_body, (shape(544, D), shape(544, D, dtype=F32), shape(1024, Q...  11.3 us
    pallas_call x1, Pallas kernels, local(): call(attend_body, (shape(T, D),) * 4 + (shape(H, T, T), shape(T, D), shap...  10.2 us
  transfers between devices with their start and end apart: 61, of which 22 were waited for; matrix products, arithmetic and copies ran while one was open for 11% of the time, Pallas kernels for 13%

profile of v1, /device:TPU:0, one launch (start us, length us, event | category | flops | bytes accessed | tf_op | source)
XLA Modules:
  0.0 449.0 jit_solution(2716122844036885930)
XLA Ops:
  1.7 5.1 %collective-permute-start.2 = (bf16[48,1536]{1,0:T(8,128)(2,1)S(1)}, bf16[48,1536]{1,0:T(8,128)(2,1)S(1)}, u32[]{:S(2)}, u32[]{:S(2)}) collective-permute-start(bf16[48,1536]{1,0:T(8,128)(2,1)S(1)} %fusion.6), channel_id=1, source_target_pairs={{0,6},{1,7},{2,4},{3,5},{4,2},{5,3},{6,0},{7,1},{8,14},{9,15},{10,... | collective-permute-start | bytes 442376 | tf_op jit(solution)/shard_map/ppermute | solution.py:485
  7.4 1.5 copy.88.routes
  11.9 3.2 shard_map.256
  15.0 1.7 collective-permute-start.16
  16.7 1.5 collective-permute-start.17
  18.2 4.8 %constant_dynamic-slice_fusion.6 = (bf16[96,1,256]{2,1,0:T(2,128)(2,1)S(1)}, bf16[96,1,256]{2,1,0:T(2,128)(2,1)S(1)}, bf16[96,1,256]{2,1,0:T(2,128)(2,1)S(1)}, b...) fusion(bf16[96,4,4096]{2,1,0:T(4,128)(2,1)} %param.30, ...), kind=kLoop, calls=%fused_computation.91 | loop fusion | bytes 1572920 | tf_op jit(solution)/shard_map/dynamic_slice | solution.py:560
  24.4 1.6 constant_dynamic-slice_fusion.1
  27.1 2.6 collective-permute-start.8
  31.7 53.3 %all-gather = bf16[8,96,16]{1,2,0:T(8,128)(2,1)S(1)} all-gather(bf16[1,96,16]{1,2,0:T(8,128)(2,1)S(1)} %bitcast.108), channel_id=1, replica_groups=mesh['rep'=4,'shard'=8] {'shard'}, dimensions={0}, use_global_device_ids=true | all-gather | bytes 27648 | tf_op jit(solution)/shard_map/all_gather | solution.py:519
  88.0 4.3 collective-permute-done.18
  95.1 3.4 collective-permute-start.27
  98.5 2.4 collective-permute-start.28
  101.0 3.6 collective-permute-start.29
  105.4 10.2 %shard_map.257 = (bf16[256,768]{1,0:T(8,128)(2,1)}, bf16[256,768]{1,0:T(8,128)(2,1)}, bf16[256,768]{1,0:T(8,128)(2,1)}, bf16[256,768]{1,0:T(8,128)(2,1)}, bf16[1...) custom-call(s32[4]{0:T(128)} %pad_add_fusion.pos, ...), custom_call_target="tpu_custom_call" | custom-call | flops 1610612736 | bytes 10485760 | tf_op jit(solution)/shard_map/pallas_call | solution.py:581
  116.6 3.9 collective-permute-done.10
  121.1 4.3 collective-permute-done.11
  125.4 5.7 %collective-permute-done.12 = bf16[64,768]{1,0:T(8,128)(2,1)S(1)} collective-permute-done((bf16[64,768]{1,0:T(8,128)(2,1)}, bf16[64,768]{1,0:T(8,128)(2,1)S(1)}, u32[]{:S(2)}, u32[]{:S(2)}) %collective-permute-start.12) | collective-permute-done | bytes 98336 | tf_op jit(solution)/shard_map/ppermute | solution.py:485
  131.3 2.1 collective-permute-start.23
  133.5 11.0 %collective-permute-done.19.g1 = bf16[256,896]{1,0:T(8,128)(2,1)S(1)} collective-permute-done((bf16[256,896]{1,0:T(8,128)(2,1)S(1)}, bf16[256,896]{1,0:T(8,128)(2,1)S(1)}, u32[]{:S(2)}, u32[]{:S(2)}) %collective-permute-start.19) | collective-permute-done | bytes 458784 | tf_op jit(solution)/shard_map/ppermute | solution.py:485
  145.7 6.5 %collective-permute-done.23.v1 = bf16[192,1024]{1,0:T(8,128)(2,1)S(1)} collective-permute-done((bf16[192,1024]{1,0:T(8,128)(2,1)S(1)}, bf16[192,1024]{1,0:T(8,128)(2,1)S(1)}, u32[]{:S(2)}, u32[]{:S(2)}) %collective-permute-start.23) | collective-permute-done | bytes 393248 | tf_op jit(solution)/shard_map/ppermute | solution.py:485
  152.2 14.8 %collective-permute-done.13.x1 = bf16[256,768]{1,0:T(8,128)(2,1)S(1)} collective-permute-done((bf16[256,768]{1,0:T(8,128)(2,1)S(1)}, bf16[256,768]{1,0:T(8,128)(2,1)S(1)}, u32[]{:S(2)}, u32[]{:S(2)}) %collective-permute-start.13) | collective-permute-done | bytes 393248 | tf_op jit(solution)/shard_map/ppermute | solution.py:485
  166.9 13.5 %collective-permute-done.24.v2 = bf16[192,1024]{1,0:T(8,128)(2,1)S(1)} collective-permute-done((bf16[192,1024]{1,0:T(8,128)(2,1)S(1)}, bf16[192,1024]{1,0:T(8,128)(2,1)S(1)}, u32[]{:S(2)}, u32[]{:S(2)}) %collective-permute-start.24) | collective-permute-done | bytes 393248 | tf_op jit(solution)/shard_map/ppermute | solution.py:485
  182.4 11.3 %shard_map.259 = (bf16[544,768]{1,0:T(8,128)(2,1)}, f32[544,768]{1,0:T(8,128)}, bf16[1024,512]{1,0:T(8,128)(2,1)}, bf16[1024,1024]{1,0:T(8,128)(2,1)}, bf16[768,...) custom-call(s32[4]{0:T(128)} %pad_add_fusion.pos, bf16[256,768]{1,0:T(8,128)(2,1)} %copy-done.21, bf16[256,768]{1,0:T(8,128)(2,1)} %copy-done.40, ...), custom_call_target="tpu_custom_call" | custom-call | flops 4026531840 | bytes 12582912 | tf_op jit(solution)/shard_map/pallas_call | solution.py:601
  193.9 8.8 %shard_map.265 = (bf16[192,1024]{1,0:T(8,128)(2,1)}, bf16[192,1024]{1,0:T(8,128)(2,1)}, bf16[192,1024]{1,0:T(8,128)(2,1)}, bf16[192,1024]{1,0:T(8,128)(2,1)}, bf...) custom-call(s32[4]{0:T(128)} %pad_add_fusion.pos, bf16[256,768]{1,0:T(8,128)(2,1)} %copy-done.21, ...), custom_call_target="tpu_custom_call" | custom-call | flops 2415919104 | bytes 12582912 | tf_op jit(solution)/shard_map/pallas_call | solution.py:620
  203.9 2.3 collective-permute-start.50
  206.2 3.5 shard_map.258
  211.0 3.3 shard_map.260
  214.3 2.5 collective-permute-start.57
  216.8 2.8 shard_map.262
  219.6 11.2 %collective-permute-done.49 = bf16[192,1024]{1,0:T(8,128)(2,1)S(1)} collective-permute-done((bf16[192,1024]{1,0:T(8,128)(2,1)}, bf16[192,1024]{1,0:T(8,128)(2,1)S(1)}, u32[]{:S(2)}, u32[]{:S(2)}) %collective-permute-start.49) | collective-permute-done | bytes 393248 | tf_op jit(solution)/shard_map/ppermute | solution.py:485
  230.9 1.5 collective-permute-done.50
  232.6 13.3 %collective-permute-done.36.got = bf16[272,768]{1,0:T(8,128)(2,1)S(1)} collective-permute-done((bf16[272,768]{1,0:T(8,128)(2,1)}, bf16[272,768]{1,0:T(8,128)(2,1)S(1)}, u32[]{:S(2)}, u32[]{:S(2)}) %collective-permute-start.36) | collective-permute-done | bytes 417824 | tf_op jit(solution)/shard_map/ppermute | solution.py:485
  246.6 2.1 shard_map.263
  248.7 1.4 collective-permute-start.37
  250.6 1.6 collective-permute-start.39
  252.3 2.6 collective-permute-done.37.r1
  257.7 18.0 %shard_map.264 = (f32[256,768]{1,0:T(8,128)}, f32[256,8]{1,0:T(8,128)}, f32[16,768]{1,0:T(8,128)}, bf16[4,192,1536]{2,1,0:T(8,128)(2,1)}, bf16[4,192,1536]{2,1,0:T(8,128)(2,1)}) custom-call(s32[4]{0:T(128)} %pad_add_fusion.pos, bf16[80,768]{1,0:T(8,128)(2,1)} %get-tuple-element.76.r0, bf16[80,768]{1,0:T(8,128)(2,1)} %copy-done.46, ...), custom_call_target="tpu_custom_call" | custom-call | flops 3422552064 | bytes 25165824 | tf_op jit(solution)/shard_map/pallas_call | solution.py:629
  275.8 1.4 collective-permute-start.52
  278.5 5.4 %collective-permute-start.31 = (bf16[256,768]{1,0:T(8,128)(2,1)}, bf16[256,768]{1,0:T(8,128)(2,1)}, u32[]{:S(2)}, u32[]{:S(2)}) collective-permute-start(bf16[256,768]{1,0:T(8,128)(2,1)} %slice.131), channel_id=1, source_target_pairs={{0,2},{1,3},{2,0},{3,1},{4,6},{5,7},{6,4},{7,5},{8,10},{9,11},{10,... | collective-permute-start | bytes 1179656 | tf_op jit(solution)/shard_map/ppermute | solution.py:485
  285.4 1.5 collective-permute-done.52
  288.7 5.3 %collective-permute-done.31 = bf16[256,768]{1,0:T(8,128)(2,1)} collective-permute-done((bf16[256,768]{1,0:T(8,128)(2,1)}, bf16[256,768]{1,0:T(8,128)(2,1)}, u32[]{:S(2)}, u32[]{:S(2)}) %collective-permute-start.31) | collective-permute-done | bytes 393248 | tf_op jit(solution)/shard_map/ppermute | solution.py:485
  297.2 8.3 %collective-permute-done.59 = bf16[2,256,768]{2,1,0:T(8,128)(2,1)S(1)} collective-permute-done((bf16[2,256,768]{2,1,0:T(8,128)(2,1)}, bf16[2,256,768]{2,1,0:T(8,128)(2,1)S(1)}, u32[]{:S(2)}, u32[]{:S(2)}) %collective-permute-start.59) | collective-permute-done | bytes 786464 | tf_op jit(solution)/shard_map/ppermute | solution.py:485
  307.7 16.7 %collective-permute-done.33.r2 = bf16[64,768]{1,0:T(8,128)(2,1)S(1)} collective-permute-done((bf16[64,768]{1,0:T(8,128)(2,1)S(1)}, bf16[64,768]{1,0:T(8,128)(2,1)S(1)}, u32[]{:S(2)}, u32[]{:S(2)}) %collective-permute-start.33) | collective-permute-done | bytes 98336 | tf_op jit(solution)/shard_map/ppermute | solution.py:485
  324.4 1.5 collective-permute-done.34.r3
  326.5 3.1 shard_map.261
  329.6 1.6 copy.108
  331.2 38.9 %psum.7 = f32[16,768]{1,0:T(8,128)} all-reduce(f32[16,768]{1,0:T(8,128)} %get-tuple-element.88), channel_id=1, replica_groups=mesh['rep'=4,'shard'=8] {'rep','shard'}, use_global_device_ids=true, to_apply=%region_0.1 | all-reduce | flops 12288 | bytes 98304 | tf_op jit(solution)/shard_map/psum | solution.py:692
  374.1 1.4 fusion.7
  375.4 1.5 pad_maximum_fusion
  377.5 2.3 add_convert_fusion
  379.9 3.2 collective-permute-start.43
  383.7 1.8 add_convert_fusion.1
  385.7 11.6 %collective-permute-done.43 = bf16[192,1536]{1,0:T(8,128)(2,1)S(1)} collective-permute-done((bf16[192,1536]{1,0:T(8,128)(2,1)S(1)}, bf16[192,1536]{1,0:T(8,128)(2,1)S(1)}, u32[]{:S(2)}, u32[]{:S(2)}) %collective-permute-start.43) | collective-permute-done | bytes 589856 | tf_op jit(solution)/shard_map/ppermute | solution.py:485
  397.3 12.4 %collective-permute-done.42 = bf16[192,1536]{1,0:T(8,128)(2,1)S(1)} collective-permute-done((bf16[192,1536]{1,0:T(8,128)(2,1)S(1)}, bf16[192,1536]{1,0:T(8,128)(2,1)S(1)}, u32[]{:S(2)}, u32[]{:S(2)}) %collective-permute-start.42) | collective-permute-done | bytes 589856 | tf_op jit(solution)/shard_map/ppermute | solution.py:485
  410.0 1.8 collective-permute-start.44
  411.8 1.5 collective-permute-start.46
  413.6 2.5 collective-permute-done.44
  416.1 5.0 %collective-permute-done.46 = bf16[48,1536]{1,0:T(8,128)(2,1)S(1)} collective-permute-done((bf16[48,1536]{1,0:T(8,128)(2,1)S(1)}, bf16[48,1536]{1,0:T(8,128)(2,1)S(1)}, u32[]{:S(2)}, u32[]{:S(2)}) %collective-permute-start.46) | collective-permute-done | bytes 147488 | tf_op jit(solution)/shard_map/ppermute | solution.py:485
  421.1 5.1 %collective-permute-done.45 = bf16[48,1536]{1,0:T(8,128)(2,1)S(1)} collective-permute-done((bf16[48,1536]{1,0:T(8,128)(2,1)S(1)}, bf16[48,1536]{1,0:T(8,128)(2,1)S(1)}, u32[]{:S(2)}, u32[]{:S(2)}) %collective-permute-start.45) | collective-permute-done | bytes 147488 | tf_op jit(solution)/shard_map/ppermute | solution.py:485
  426.2 1.9 collective-permute-start.47
  428.4 3.7 copy.110
  433.2 3.9 shard_map.266
  437.3 2.6 convert_bitcast_fusion
  439.9 6.8 %copy.109 = f32[96,4,4096]{2,1,0:T(4,128)} copy(f32[96,4,4096]{2,0,1:T(8,128)S(1)} %convert_bitcast_fusion) | data formatting | bytes 12582912
  (247 shorter events, 47.6 us)
Async XLA Ops:
  1.7 24.4 %collective-permute-start.2 = (bf16[48,1536]{1,0:T(8,128)(2,1)S(1)}, bf16[48,1536]{1,0:T(8,128)(2,1)S(1)}, u32[]{:S(2)}, u32[]{:S(2)}) collective-permute-start(bf16[48,1536]{1,0:T(8,128)(2,1)S(1)} %fusion.6), channel_id=1, source_target_pairs={{0,6},{1,7},{2,4},{3,5},{4,2},{5,3},{6,0},{7,1},{8,14},{9,15},{10,... | collective-permute-start | bytes 442376 | tf_op jit(solution)/shard_map/ppermute | solution.py:485
  6.8 19.3 %collective-permute-start.1 = (bf16[48,1536]{1,0:T(8,128)(2,1)S(1)}, bf16[48,1536]{1,0:T(8,128)(2,1)S(1)}, u32[]{:S(2)}, u32[]{:S(2)}) collective-permute-start(bf16[48,1536]{1,0:T(8,128)(2,1)S(1)} %fusion.6), channel_id=1, source_target_pairs={{0,4},{1,5},{2,6},{3,7},{4,0},{5,1},{6,2},{7,3},{8,12},{9,13},{10,... | collective-permute-start | bytes 442376 | tf_op jit(solution)/shard_map/ppermute | solution.py:485
  6.8 19.3 %collective-permute-start = (bf16[48,1536]{1,0:T(8,128)(2,1)S(1)}, bf16[48,1536]{1,0:T(8,128)(2,1)S(1)}, u32[]{:S(2)}, u32[]{:S(2)}) collective-permute-start(bf16[48,1536]{1,0:T(8,128)(2,1)S(1)} %fusion.6), channel_id=1, source_target_pairs={{0,2},{1,3},{2,0},{3,1},{4,6},{5,7},{6,4},{7,5},{8,10},{9,11},{10,... | collective-permute-start | bytes 442376 | tf_op jit(solution)/shard_map/ppermute | solution.py:485
  15.0 14.8 %collective-permute-start.16 = (bf16[64,896]{1,0:T(8,128)(2,1)}, bf16[64,896]{1,0:T(8,128)(2,1)}, u32[]{:S(2)}, u32[]{:S(2)}) collective-permute-start(bf16[64,896]{1,0:T(8,128)(2,1)} %get-tuple-element.65), channel_id=1, source_target_pairs={{0,1},{1,0},{2,3},{3,2},{4,5},{5,4},{6,7},{7,6},{8,9},{9,8},{10,11... | collective-permute-start | bytes 344072 | tf_op jit(solution)/shard_map/ppermute | solution.py:485
  16.7 69.1 %collective-permute-start.17 = (bf16[64,896]{1,0:T(8,128)(2,1)}, bf16[64,896]{1,0:T(8,128)(2,1)}, u32[]{:S(2)}, u32[]{:S(2)}) collective-permute-start(bf16[64,896]{1,0:T(8,128)(2,1)} %get-tuple-element.66), channel_id=1, source_target_pairs={{0,16},{1,17},{2,18},{3,19},{4,20},{5,21},{6,22},{7,23},{8,24},{9,... | collective-permute-start | bytes 344072 | tf_op jit(solution)/shard_map/ppermute | solution.py:485
  26.2 66.2 %copy-start.10 = (bf16[192,1536]{1,0:T(8,128)(2,1)}, bf16[192,1536]{1,0:T(8,128)(2,1)S(1)}, u32[]{:S(2)}) copy-start(bf16[192,1536]{1,0:T(8,128)(2,1)S(1)} %pad_maximum_fusion.4.w0) | copy-start | bytes 1769476
  26.2 66.2 %collective-permute-start.4 = (bf16[192,1536]{1,0:T(8,128)(2,1)S(1)}, bf16[192,1536]{1,0:T(8,128)(2,1)}, u32[]{:S(2)}, u32[]{:S(2)}) collective-permute-start(bf16[192,1536]{1,0:T(8,128)(2,1)S(1)} %pad_maximum_fusion.4.w0), channel_id=1, source_target_pairs={{0,1},{1,0},{2,3},{3,2},{4,5},{5,4},{6,7},{7,6},{8,9},{9,8},{10,11... | collective-permute-start | bytes 1769480 | tf_op jit(solution)/shard_map/ppermute | solution.py:485
  26.7 66.1 %collective-permute-start.6 = (bf16[192,1536]{1,0:T(8,128)(2,1)S(1)}, bf16[192,1536]{1,0:T(8,128)(2,1)}, u32[]{:S(2)}, u32[]{:S(2)}) collective-permute-start(bf16[192,1536]{1,0:T(8,128)(2,1)S(1)} %pad_maximum_fusion.4.w0), channel_id=1, source_target_pairs={{0,16},{1,17},{2,18},{3,19},{4,20},{5,21},{6,22},{7,23},{8,24},{9,... | collective-permute-start | bytes 1769480 | tf_op jit(solution)/shard_map/ppermute | solution.py:485
  27.1 65.8 %collective-permute-start.8 = (bf16[192,1536]{1,0:T(8,128)(2,1)S(1)}, bf16[192,1536]{1,0:T(8,128)(2,1)}, u32[]{:S(2)}, u32[]{:S(2)}) collective-permute-start(bf16[192,1536]{1,0:T(8,128)(2,1)S(1)} %pad_maximum_fusion.4.w0), channel_id=1, source_target_pairs={{0,17},{1,16},{2,19},{3,18},{4,21},{5,20},{6,23},{7,22},{8,25},{9,... | collective-permute-start | bytes 1769480 | tf_op jit(solution)/shard_map/ppermute | solution.py:485
  29.8 64.5 %collective-permute-start.22 = (bf16[2,96,1024]{2,1,0:T(8,128)(2,1)S(1)}, bf16[2,96,1024]{2,1,0:T(8,128)(2,1)S(1)}, u32[]{:S(2)}, u32[]{:S(2)}) collective-permute-start(bf16[2,96,1024]{2,1,0:T(8,128)(2,1)S(1)} %pad_maximum_fusion.6), channel_id=1, source_target_pairs={{0,1},{1,0},{2,3},{3,2},{4,5},{5,4},{6,7},{7,6},{8,9},{9,8},{10,11... | collective-permute-start | bytes 1179656 | tf_op jit(solution)/shard_map/ppermute | solution.py:485
  86.6 5.7 %collective-permute-start.18 = (bf16[64,896]{1,0:T(8,128)(2,1)S(1)}, bf16[64,896]{1,0:T(8,128)(2,1)S(1)}, u32[]{:S(2)}, u32[]{:S(2)}) collective-permute-start(bf16[64,896]{1,0:T(8,128)(2,1)S(1)} %copy-done.49), channel_id=1, source_target_pairs={{0,17},{1,16},{2,19},{3,18},{4,21},{5,20},{6,23},{7,22},{8,25},{9,... | collective-permute-start | bytes 344072 | tf_op jit(solution)/shard_map/ppermute | solution.py:485
  92.3 2.8 collective-permute-start.3
  92.3 6.2 %collective-permute-start.5 = (bf16[192,1536]{1,0:T(8,128)(2,1)}, bf16[192,1536]{1,0:T(8,128)(2,1)S(1)}, u32[]{:S(2)}, u32[]{:S(2)}) collective-permute-start(bf16[192,1536]{1,0:T(8,128)(2,1)} %collective-permute-done.4.w2), channel_id=1, source_target_pairs={{0,8},{1,9},{2,10},{3,11},{4,12},{5,13},{6,14},{7,15},{8,0},{9,1},... | collective-permute-start | bytes 1769480 | tf_op jit(solution)/shard_map/ppermute | solution.py:485
  92.8 8.1 %collective-permute-start.7 = (bf16[192,1536]{1,0:T(8,128)(2,1)}, bf16[192,1536]{1,0:T(8,128)(2,1)S(1)}, u32[]{:S(2)}, u32[]{:S(2)}) collective-permute-start(bf16[192,1536]{1,0:T(8,128)(2,1)} %collective-permute-done.6.w4), channel_id=1, source_target_pairs={{0,8},{1,9},{2,10},{3,11},{4,12},{5,13},{6,14},{7,15},{8,0},{9,1},... | collective-permute-start | bytes 1769480 | tf_op jit(solution)/shard_map/ppermute | solution.py:485
  92.9 11.7 %collective-permute-start.9 = (bf16[192,1536]{1,0:T(8,128)(2,1)}, bf16[192,1536]{1,0:T(8,128)(2,1)S(1)}, u32[]{:S(2)}, u32[]{:S(2)}) collective-permute-start(bf16[192,1536]{1,0:T(8,128)(2,1)} %collective-permute-done.8.w6), channel_id=1, source_target_pairs={{0,8},{1,9},{2,10},{3,11},{4,12},{5,13},{6,14},{7,15},{8,0},{9,1},... | collective-permute-start | bytes 1769480 | tf_op jit(solution)/shard_map/ppermute | solution.py:485
  94.3 36.8 %collective-permute-start.26 = (bf16[256,768]{1,0:T(8,128)(2,1)S(1)}, bf16[256,768]{1,0:T(8,128)(2,1)S(1)}, u32[]{:S(2)}, u32[]{:S(2)}) collective-permute-start(bf16[256,768]{1,0:T(8,128)(2,1)S(1)} %bitcast.102), channel_id=1, source_target_pairs={{0,0},{1,1},{4,2},{5,3},{10,8},{11,9},{14,10},{15,11},{16,16},{17,... | collective-permute-start | bytes 1179656 | tf_op jit(solution)/shard_map/ppermute | solution.py:579
  95.1 36.1 %collective-permute-start.27 = (bf16[256,768]{1,0:T(8,128)(2,1)S(1)}, bf16[256,768]{1,0:T(8,128)(2,1)S(1)}, u32[]{:S(2)}, u32[]{:S(2)}) collective-permute-start(bf16[256,768]{1,0:T(8,128)(2,1)S(1)} %bitcast.103), channel_id=1, source_target_pairs={{0,4},{1,5},{4,6},{5,7},{10,12},{11,13},{14,14},{15,15},{16,20},{1... | collective-permute-start | bytes 1179656 | tf_op jit(solution)/shard_map/ppermute | solution.py:579
  98.5 34.8 %collective-permute-start.28 = (bf16[256,768]{1,0:T(8,128)(2,1)S(1)}, bf16[256,768]{1,0:T(8,128)(2,1)S(1)}, u32[]{:S(2)}, u32[]{:S(2)}) collective-permute-start(bf16[256,768]{1,0:T(8,128)(2,1)S(1)} %bitcast.100), channel_id=1, source_target_pairs={{1,0},{0,1},{5,2},{4,3},{11,8},{10,9},{15,10},{14,11},{17,16},{16,... | collective-permute-start | bytes 1179656 | tf_op jit(solution)/shard_map/ppermute | solution.py:579
  101.0 43.6 %collective-permute-start.29 = (bf16[256,768]{1,0:T(8,128)(2,1)S(1)}, bf16[256,768]{1,0:T(8,128)(2,1)S(1)}, u32[]{:S(2)}, u32[]{:S(2)}) collective-permute-start(bf16[256,768]{1,0:T(8,128)(2,1)S(1)} %bitcast.101), channel_id=1, source_target_pairs={{1,4},{0,5},{5,6},{4,7},{11,12},{10,13},{15,14},{14,15},{17,20},{1... | collective-permute-start | bytes 1179656 | tf_op jit(solution)/shard_map/ppermute | solution.py:579
  115.7 4.9 %collective-permute-start.10 = (bf16[64,768]{1,0:T(8,128)(2,1)}, bf16[64,768]{1,0:T(8,128)(2,1)S(1)}, u32[]{:S(2)}, u32[]{:S(2)}) collective-permute-start(bf16[64,768]{1,0:T(8,128)(2,1)} %get-tuple-element.61), channel_id=1, source_target_pairs={{0,1},{1,0},{2,3},{3,2},{4,5},{5,4},{6,7},{7,6},{8,9},{9,8},{10,11... | collective-permute-start | bytes 294920 | tf_op jit(solution)/shard_map/ppermute | solution.py:485
  120.6 4.8 %collective-permute-start.11 = (bf16[64,768]{1,0:T(8,128)(2,1)}, bf16[64,768]{1,0:T(8,128)(2,1)S(1)}, u32[]{:S(2)}, u32[]{:S(2)}) collective-permute-start(bf16[64,768]{1,0:T(8,128)(2,1)} %get-tuple-element.62), channel_id=1, source_target_pairs={{0,16},{1,17},{2,18},{3,19},{4,20},{5,21},{6,22},{7,23},{8,24},{9,... | collective-permute-start | bytes 294920 | tf_op jit(solution)/shard_map/ppermute | solution.py:485
  125.4 5.7 %collective-permute-start.12 = (bf16[64,768]{1,0:T(8,128)(2,1)}, bf16[64,768]{1,0:T(8,128)(2,1)S(1)}, u32[]{:S(2)}, u32[]{:S(2)}) collective-permute-start(bf16[64,768]{1,0:T(8,128)(2,1)} %get-tuple-element.63), channel_id=1, source_target_pairs={{0,17},{1,16},{2,19},{3,18},{4,21},{5,20},{6,23},{7,22},{8,25},{9,... | collective-permute-start | bytes 294920 | tf_op jit(solution)/shard_map/ppermute | solution.py:485
  131.1 13.4 %collective-permute-start.19 = (bf16[256,896]{1,0:T(8,128)(2,1)S(1)}, bf16[256,896]{1,0:T(8,128)(2,1)S(1)}, u32[]{:S(2)}, u32[]{:S(2)}) collective-permute-start(bf16[256,896]{1,0:T(8,128)(2,1)S(1)} %constant_dynamic-update-slice_fusion.4.g0), channel_id=1, source_target_pairs={{0,2},{1,3},{2,0},{3,1},{4,6},{5,7},{6,4},{7,5},{8,10},{9,11},{10,... | collective-permute-start | bytes 1376264 | tf_op jit(solution)/shard_map/ppermute | solution.py:485
  131.1 49.4 %copy-start.21 = (bf16[256,768]{1,0:T(8,128)(2,1)}, bf16[256,768]{1,0:T(8,128)(2,1)S(1)}, u32[]{:S(2)}) copy-start(bf16[256,768]{1,0:T(8,128)(2,1)S(1)} %constant_dynamic-update-slice_fusion.x0) | copy-start | bytes 1179652
  131.2 49.4 %copy-start.34 = (bf16[256,768]{1,0:T(8,128)(2,1)}, bf16[256,768]{1,0:T(8,128)(2,1)S(1)}, u32[]{:S(2)}) copy-start(bf16[256,768]{1,0:T(8,128)(2,1)S(1)} %collective-permute-done.26.e0) | copy-start | bytes 1179652
  131.2 13.5 %collective-permute-start.20 = (bf16[256,896]{1,0:T(8,128)(2,1)S(1)}, bf16[256,896]{1,0:T(8,128)(2,1)S(1)}, u32[]{:S(2)}, u32[]{:S(2)}) collective-permute-start(bf16[256,896]{1,0:T(8,128)(2,1)S(1)} %constant_dynamic-update-slice_fusion.4.g0), channel_id=1, source_target_pairs={{0,8},{1,9},{2,10},{3,11},{4,12},{5,13},{6,14},{7,15},{8,0},{9,1},... | collective-permute-start | bytes 1376264 | tf_op jit(solution)/shard_map/ppermute | solution.py:485
  131.3 20.9 %collective-permute-start.23 = (bf16[192,1024]{1,0:T(8,128)(2,1)S(1)}, bf16[192,1024]{1,0:T(8,128)(2,1)S(1)}, u32[]{:S(2)}, u32[]{:S(2)}) collective-permute-start(bf16[192,1024]{1,0:T(8,128)(2,1)S(1)} %pad_maximum_fusion.8), channel_id=1, source_target_pairs={{0,2},{1,3},{2,0},{3,1},{4,6},{5,7},{6,4},{7,5},{8,10},{9,11},{10,... | collective-permute-start | bytes 1179656 | tf_op jit(solution)/shard_map/ppermute | solution.py:485
  133.3 33.6 %collective-permute-start.13 = (bf16[256,768]{1,0:T(8,128)(2,1)S(1)}, bf16[256,768]{1,0:T(8,128)(2,1)S(1)}, u32[]{:S(2)}, u32[]{:S(2)}) collective-permute-start(bf16[256,768]{1,0:T(8,128)(2,1)S(1)} %constant_dynamic-update-slice_fusion.x0), channel_id=1, source_target_pairs={{0,2},{1,3},{2,0},{3,1},{4,6},{5,7},{6,4},{7,5},{8,10},{9,11},{10,... | collective-permute-start | bytes 1179656 | tf_op jit(solution)/shard_map/ppermute | solution.py:485
  144.5 36.0 %collective-permute-start.21 = (bf16[256,896]{1,0:T(8,128)(2,1)S(1)}, bf16[256,896]{1,0:T(8,128)(2,1)S(1)}, u32[]{:S(2)}, u32[]{:S(2)}) collective-permute-start(bf16[256,896]{1,0:T(8,128)(2,1)S(1)} %collective-permute-done.19.g1), channel_id=1, source_target_pairs={{0,8},{1,9},{2,10},{3,11},{4,12},{5,13},{6,14},{7,15},{8,0},{9,1},... | collective-permute-start | bytes 1376264 | tf_op jit(solution)/shard_map/ppermute | solution.py:485
  144.6 35.9 %collective-permute-start.25 = (bf16[192,1024]{1,0:T(8,128)(2,1)S(1)}, bf16[192,1024]{1,0:T(8,128)(2,1)S(1)}, u32[]{:S(2)}, u32[]{:S(2)}) collective-permute-start(bf16[192,1024]{1,0:T(8,128)(2,1)S(1)} %pad_maximum_fusion.8), channel_id=1, source_target_pairs={{0,6},{1,7},{2,4},{3,5},{4,2},{5,3},{6,0},{7,1},{8,14},{9,15},{10,... | collective-permute-start | bytes 1179656 | tf_op jit(solution)/shard_map/ppermute | solution.py:485
  144.7 35.8 %collective-permute-start.24 = (bf16[192,1024]{1,0:T(8,128)(2,1)S(1)}, bf16[192,1024]{1,0:T(8,128)(2,1)S(1)}, u32[]{:S(2)}, u32[]{:S(2)}) collective-permute-start(bf16[192,1024]{1,0:T(8,128)(2,1)S(1)} %pad_maximum_fusion.7.v0), channel_id=1, source_target_pairs={{0,4},{1,5},{2,6},{3,7},{4,0},{5,1},{6,2},{7,3},{8,12},{9,13},{10,... | collective-permute-start | bytes 1179656 | tf_op jit(solution)/shard_map/ppermute | solution.py:485
  152.2 28.3 %collective-permute-start.14 = (bf16[256,768]{1,0:T(8,128)(2,1)S(1)}, bf16[256,768]{1,0:T(8,128)(2,1)S(1)}, u32[]{:S(2)}, u32[]{:S(2)}) collective-permute-start(bf16[256,768]{1,0:T(8,128)(2,1)S(1)} %constant_dynamic-update-slice_fusion.x0), channel_id=1, source_target_pairs={{0,8},{1,9},{2,10},{3,11},{4,12},{5,13},{6,14},{7,15},{8,0},{9,1},... | collective-permute-start | bytes 1179656 | tf_op jit(solution)/shard_map/ppermute | solution.py:485
  166.9 13.6 %collective-permute-start.15 = (bf16[256,768]{1,0:T(8,128)(2,1)S(1)}, bf16[256,768]{1,0:T(8,128)(2,1)S(1)}, u32[]{:S(2)}, u32[]{:S(2)}) collective-permute-start(bf16[256,768]{1,0:T(8,128)(2,1)S(1)} %collective-permute-done.13.x1), channel_id=1, source_target_pairs={{0,8},{1,9},{2,10},{3,11},{4,12},{5,13},{6,14},{7,15},{8,0},{9,1},... | collective-permute-start | bytes 1179656 | tf_op jit(solution)/shard_map/ppermute | solution.py:485
  193.8 20.5 %collective-permute-start.35 = (bf16[544,768]{1,0:T(8,128)(2,1)}, bf16[544,768]{1,0:T(8,128)(2,1)S(1)}, u32[]{:S(2)}, u32[]{:S(2)}) collective-permute-start(bf16[544,768]{1,0:T(8,128)(2,1)} %get-tuple-element.73), channel_id=1, source_target_pairs={{0,8},{1,9},{2,10},{3,11},{4,12},{5,13},{6,14},{7,15},{8,0},{9,1},... | collective-permute-start | bytes 2506760 | tf_op jit(solution)/shard_map/ppermute | solution.py:485
  202.6 28.1 %collective-permute-start.49 = (bf16[192,1024]{1,0:T(8,128)(2,1)}, bf16[192,1024]{1,0:T(8,128)(2,1)S(1)}, u32[]{:S(2)}, u32[]{:S(2)}) collective-permute-start(bf16[192,1024]{1,0:T(8,128)(2,1)} %get-tuple-element.93), channel_id=1, source_target_pairs={{0,4},{1,5},{2,6},{3,7},{4,0},{5,1},{6,2},{7,3},{8,12},{9,13},{10,... | collective-permute-start | bytes 1179656 | tf_op jit(solution)/shard_map/ppermute | solution.py:485
  202.7 28.2 %collective-permute-start.51 = (bf16[192,1024]{1,0:T(8,128)(2,1)}, bf16[192,1024]{1,0:T(8,128)(2,1)S(1)}, u32[]{:S(2)}, u32[]{:S(2)}) collective-permute-start(bf16[192,1024]{1,0:T(8,128)(2,1)} %get-tuple-element.95), channel_id=1, source_target_pairs={{0,6},{1,7},{2,4},{3,5},{4,2},{5,3},{6,0},{7,1},{8,14},{9,15},{10,... | collective-permute-start | bytes 1179656 | tf_op jit(solution)/shard_map/ppermute | solution.py:485
  203.9 28.5 %collective-permute-start.50 = (bf16[192,1024]{1,0:T(8,128)(2,1)}, bf16[192,1024]{1,0:T(8,128)(2,1)S(1)}, u32[]{:S(2)}, u32[]{:S(2)}) collective-permute-start(bf16[192,1024]{1,0:T(8,128)(2,1)} %get-tuple-element.94), channel_id=1, source_target_pairs={{0,2},{1,3},{2,0},{3,1},{4,6},{5,7},{6,4},{7,5},{8,10},{9,11},{10,... | collective-permute-start | bytes 1179656 | tf_op jit(solution)/shard_map/ppermute | solution.py:485
  209.7 66.1 %collective-permute-start.58 = (bf16[256,768]{1,0:T(8,128)(2,1)S(1)}, bf16[256,768]{1,0:T(8,128)(2,1)S(1)}, u32[]{:S(2)}, u32[]{:S(2)}) collective-permute-start(bf16[256,768]{1,0:T(8,128)(2,1)S(1)} %copy-done.38), channel_id=1, source_target_pairs={{4,1},{5,0},{6,5},{7,4},{12,11},{13,10},{14,15},{15,14},{20,17},{2... | collective-permute-start | bytes 1179656 | tf_op jit(solution)/shard_map/ppermute | solution.py:665
  214.3 62.9 %collective-permute-start.57 = (bf16[256,768]{1,0:T(8,128)(2,1)S(1)}, bf16[256,768]{1,0:T(8,128)(2,1)S(1)}, u32[]{:S(2)}, u32[]{:S(2)}) collective-permute-start(bf16[256,768]{1,0:T(8,128)(2,1)S(1)} %copy-done.38), channel_id=1, source_target_pairs={{0,1},{1,0},{2,5},{3,4},{8,11},{9,10},{10,15},{11,14},{16,17},{17,... | collective-permute-start | bytes 1179656 | tf_op jit(solution)/shard_map/ppermute | solution.py:665
  230.8 15.1 %collective-permute-start.36 = (bf16[272,768]{1,0:T(8,128)(2,1)}, bf16[272,768]{1,0:T(8,128)(2,1)S(1)}, u32[]{:S(2)}, u32[]{:S(2)}) collective-permute-start(bf16[272,768]{1,0:T(8,128)(2,1)} %get-tuple-element.75), channel_id=1, source_target_pairs={{0,2},{1,3},{2,0},{3,1},{4,6},{5,7},{6,4},{7,5},{8,10},{9,11},{10,... | collective-permute-start | bytes 1253384 | tf_op jit(solution)/shard_map/ppermute | solution.py:485
  248.7 6.1 %collective-permute-start.37 = (bf16[80,768]{1,0:T(8,128)(2,1)}, bf16[80,768]{1,0:T(8,128)(2,1)S(1)}, u32[]{:S(2)}, u32[]{:S(2)}) collective-permute-start(bf16[80,768]{1,0:T(8,128)(2,1)} %get-tuple-element.77), channel_id=1, source_target_pairs={{0,1},{1,0},{2,3},{3,2},{4,5},{5,4},{6,7},{7,6},{8,9},{9,8},{10,11... | collective-permute-start | bytes 368648 | tf_op jit(solution)/shard_map/ppermute | solution.py:485
  250.1 6.1 %collective-permute-start.38 = (bf16[80,768]{1,0:T(8,128)(2,1)}, bf16[80,768]{1,0:T(8,128)(2,1)S(1)}, u32[]{:S(2)}, u32[]{:S(2)}) collective-permute-start(bf16[80,768]{1,0:T(8,128)(2,1)} %get-tuple-element.78), channel_id=1, source_target_pairs={{0,16},{1,17},{2,18},{3,19},{4,20},{5,21},{6,22},{7,23},{8,24},{9,... | collective-permute-start | bytes 368648 | tf_op jit(solution)/shard_map/ppermute | solution.py:485
  250.6 6.5 %collective-permute-start.39 = (bf16[80,768]{1,0:T(8,128)(2,1)}, bf16[80,768]{1,0:T(8,128)(2,1)S(1)}, u32[]{:S(2)}, u32[]{:S(2)}) collective-permute-start(bf16[80,768]{1,0:T(8,128)(2,1)} %get-tuple-element.79), channel_id=1, source_target_pairs={{0,17},{1,16},{2,19},{3,18},{4,21},{5,20},{6,23},{7,22},{8,25},{9,... | collective-permute-start | bytes 368648 | tf_op jit(solution)/shard_map/ppermute | solution.py:485
  254.9 22.5 %collective-permute-start.56 = (bf16[256,768]{1,0:T(8,128)(2,1)S(1)}, bf16[256,768]{1,0:T(8,128)(2,1)S(1)}, u32[]{:S(2)}, u32[]{:S(2)}) collective-permute-start(bf16[256,768]{1,0:T(8,128)(2,1)S(1)} %copy-done.35), channel_id=1, source_target_pairs={{4,0},{5,1},{6,4},{7,5},{12,10},{13,11},{14,14},{15,15},{20,16},{2... | collective-permute-start | bytes 1179656 | tf_op jit(solution)/shard_map/ppermute | solution.py:665
  256.2 21.2 %collective-permute-start.55 = (bf16[256,768]{1,0:T(8,128)(2,1)S(1)}, bf16[256,768]{1,0:T(8,128)(2,1)S(1)}, u32[]{:S(2)}, u32[]{:S(2)}) collective-permute-start(bf16[256,768]{1,0:T(8,128)(2,1)S(1)} %copy-done.35), channel_id=1, source_target_pairs={{0,0},{1,1},{2,4},{3,5},{8,10},{9,11},{10,14},{11,15},{16,16},{17,... | collective-permute-start | bytes 1179656 | tf_op jit(solution)/shard_map/ppermute | solution.py:665
  257.1 20.4 %collective-permute-start.30 = (bf16[512,768]{1,0:T(8,128)(2,1)S(1)}, bf16[512,768]{1,0:T(8,128)(2,1)S(1)}, u32[]{:S(2)}, u32[]{:S(2)}) collective-permute-start(bf16[512,768]{1,0:T(8,128)(2,1)S(1)} %copy-done.26), channel_id=1, source_target_pairs={{0,8},{1,9},{2,10},{3,11},{4,12},{5,13},{6,14},{7,15},{8,0},{9,1},... | collective-permute-start | bytes 2359304 | tf_op jit(solution)/shard_map/ppermute | solution.py:485
  275.8 11.1 %collective-permute-start.52 = (bf16[2,96,1024]{2,1,0:T(8,128)(2,1)S(1)}, bf16[2,96,1024]{2,1,0:T(8,128)(2,1)S(1)}, u32[]{:S(2)}, u32[]{:S(2)}) collective-permute-start(bf16[2,96,1024]{2,1,0:T(8,128)(2,1)S(1)} %get-tuple-element.176), channel_id=1, source_target_pairs={{0,1},{1,0},{2,3},{3,2},{4,5},{5,4},{6,7},{7,6},{8,9},{9,8},{10,11... | collective-permute-start | bytes 1179656 | tf_op jit(solution)/shard_map/ppermute | solution.py:485
  277.2 99.8 %collective-permute-start.40 = (bf16[4,192,1536]{2,1,0:T(8,128)(2,1)}, bf16[4,192,1536]{2,1,0:T(8,128)(2,1)}, u32[]{:S(2)}, u32[]{:S(2)}) collective-permute-start(bf16[4,192,1536]{2,1,0:T(8,128)(2,1)} %get-tuple-element.90), channel_id=1, source_target_pairs={{0,8},{1,9},{2,10},{3,11},{4,12},{5,13},{6,14},{7,15},{8,0},{9,1},... | collective-permute-start | bytes 7077896 | tf_op jit(solution)/shard_map/ppermute | solution.py:485
  278.5 15.5 %collective-permute-start.31 = (bf16[256,768]{1,0:T(8,128)(2,1)}, bf16[256,768]{1,0:T(8,128)(2,1)}, u32[]{:S(2)}, u32[]{:S(2)}) collective-permute-start(bf16[256,768]{1,0:T(8,128)(2,1)} %slice.131), channel_id=1, source_target_pairs={{0,2},{1,3},{2,0},{3,1},{4,6},{5,7},{6,4},{7,5},{8,10},{9,11},{10,... | collective-permute-start | bytes 1179656 | tf_op jit(solution)/shard_map/ppermute | solution.py:485
  284.9 20.6 %collective-permute-start.59 = (bf16[2,256,768]{2,1,0:T(8,128)(2,1)}, bf16[2,256,768]{2,1,0:T(8,128)(2,1)S(1)}, u32[]{:S(2)}, u32[]{:S(2)}) collective-permute-start(bf16[2,256,768]{2,1,0:T(8,128)(2,1)} %get-tuple-element.174), channel_id=1, source_target_pairs={{0,16},{1,17},{2,18},{3,19},{4,20},{5,21},{6,22},{7,23},{8,24},{9,... | collective-permute-start | bytes 2359304 | tf_op jit(solution)/shard_map/ppermute | solution.py:485
  287.7 87.7 %collective-permute-start.53 = (bf16[4,96,1024]{2,1,0:T(8,128)(2,1)S(1)}, bf16[4,96,1024]{2,1,0:T(8,128)(2,1)S(1)}, u32[]{:S(2)}, u32[]{:S(2)}) collective-permute-start(bf16[4,96,1024]{2,1,0:T(8,128)(2,1)S(1)} %pad_maximum_fusion.2.own), channel_id=1, source_target_pairs={{0,16},{1,17},{2,18},{3,19},{4,20},{5,21},{6,22},{7,23},{8,24},{9,... | collective-permute-start | bytes 2359304 | tf_op jit(solution)/shard_map/ppermute | solution.py:485
  295.7 11.9 %collective-permute-start.32 = (bf16[64,768]{1,0:T(8,128)(2,1)S(1)}, bf16[64,768]{1,0:T(8,128)(2,1)S(1)}, u32[]{:S(2)}, u32[]{:S(2)}) collective-permute-start(bf16[64,768]{1,0:T(8,128)(2,1)S(1)} %get-tuple-element.184), channel_id=1, source_target_pairs={{0,1},{1,0},{2,3},{3,2},{4,5},{5,4},{6,7},{7,6},{8,9},{9,8},{10,11... | collective-permute-start | bytes 294920 | tf_op jit(solution)/shard_map/ppermute | solution.py:485
  296.4 28.0 %collective-permute-start.33 = (bf16[64,768]{1,0:T(8,128)(2,1)S(1)}, bf16[64,768]{1,0:T(8,128)(2,1)S(1)}, u32[]{:S(2)}, u32[]{:S(2)}) collective-permute-start(bf16[64,768]{1,0:T(8,128)(2,1)S(1)} %get-tuple-element.183), channel_id=1, source_target_pairs={{0,16},{1,17},{2,18},{3,19},{4,20},{5,21},{6,22},{7,23},{8,24},{9,... | collective-permute-start | bytes 294920 | tf_op jit(solution)/shard_map/ppermute | solution.py:485
  305.5 20.4 %collective-permute-start.34 = (bf16[64,768]{1,0:T(8,128)(2,1)S(1)}, bf16[64,768]{1,0:T(8,128)(2,1)S(1)}, u32[]{:S(2)}, u32[]{:S(2)}) collective-permute-start(bf16[64,768]{1,0:T(8,128)(2,1)S(1)} %get-tuple-element.182), channel_id=1, source_target_pairs={{0,17},{1,16},{2,19},{3,18},{4,21},{5,20},{6,23},{7,22},{8,25},{9,... | collective-permute-start | bytes 294920 | tf_op jit(solution)/shard_map/ppermute | solution.py:485
  307.7 76.1 %collective-permute-start.60 = (bf16[2,2,256,768]{3,2,1,0:T(8,128)(2,1)}, bf16[2,2,256,768]{3,2,1,0:T(8,128)(2,1)}, u32[]{:S(2)}, u32[]{:S(2)}) collective-permute-start(bf16[2,2,256,768]{3,2,1,0:T(8,128)(2,1)} %pad_maximum_fusion.1), channel_id=1, source_target_pairs={{0,8},{1,9},{2,10},{3,11},{4,12},{5,13},{6,14},{7,15},{8,0},{9,1},... | collective-permute-start | bytes 4718600 | tf_op jit(solution)/shard_map/ppermute | solution.py:485
  377.0 55.1 %collective-permute-start.54 = (bf16[8,96,1024]{2,1,0:T(8,128)(2,1)S(1)}, bf16[8,96,1024]{2,1,0:T(8,128)(2,1)S(1)}, u32[]{:S(2)}, u32[]{:S(2)}) collective-permute-start(bf16[8,96,1024]{2,1,0:T(8,128)(2,1)S(1)} %pad_maximum_fusion), channel_id=1, source_target_pairs={{0,8},{1,9},{2,10},{3,11},{4,12},{5,13},{6,14},{7,15},{8,0},{9,1},... | collective-permute-start | bytes 4718600 | tf_op jit(solution)/shard_map/ppermute | solution.py:485
  379.9 17.3 %collective-permute-start.43 = (bf16[192,1536]{1,0:T(8,128)(2,1)S(1)}, bf16[192,1536]{1,0:T(8,128)(2,1)S(1)}, u32[]{:S(2)}, u32[]{:S(2)}) collective-permute-start(bf16[192,1536]{1,0:T(8,128)(2,1)S(1)} %get-tuple-element.163), channel_id=1, source_target_pairs={{0,17},{1,16},{2,19},{3,18},{4,21},{5,20},{6,23},{7,22},{8,25},{9,... | collective-permute-start | bytes 1769480 | tf_op jit(solution)/shard_map/ppermute | solution.py:485
  383.1 26.5 %collective-permute-start.42 = (bf16[192,1536]{1,0:T(8,128)(2,1)S(1)}, bf16[192,1536]{1,0:T(8,128)(2,1)S(1)}, u32[]{:S(2)}, u32[]{:S(2)}) collective-permute-start(bf16[192,1536]{1,0:T(8,128)(2,1)S(1)} %get-tuple-element.164), channel_id=1, source_target_pairs={{0,16},{1,17},{2,18},{3,19},{4,20},{5,21},{6,22},{7,23},{8,24},{9,... | collective-permute-start | bytes 1769480 | tf_op jit(solution)/shard_map/ppermute | solution.py:485
  383.7 25.9 %collective-permute-start.41 = (bf16[192,1536]{1,0:T(8,128)(2,1)S(1)}, bf16[192,1536]{1,0:T(8,128)(2,1)S(1)}, u32[]{:S(2)}, u32[]{:S(2)}) collective-permute-start(bf16[192,1536]{1,0:T(8,128)(2,1)S(1)} %get-tuple-element.162), channel_id=1, source_target_pairs={{0,1},{1,0},{2,3},{3,2},{4,5},{5,4},{6,7},{7,6},{8,9},{9,8},{10,11... | collective-permute-start | bytes 1769480 | tf_op jit(solution)/shard_map/ppermute | solution.py:485
  410.0 6.1 %collective-permute-start.44 = (bf16[48,1536]{1,0:T(8,128)(2,1)S(1)}, bf16[48,1536]{1,0:T(8,128)(2,1)S(1)}, u32[]{:S(2)}, u32[]{:S(2)}) collective-permute-start(bf16[48,1536]{1,0:T(8,128)(2,1)S(1)} %get-tuple-element.181), channel_id=1, source_target_pairs={{0,2},{1,3},{2,0},{3,1},{4,6},{5,7},{6,4},{7,5},{8,10},{9,11},{10,... | collective-permute-start | bytes 442376 | tf_op jit(solution)/shard_map/ppermute | solution.py:485
  411.8 9.3 %collective-permute-start.46 = (bf16[48,1536]{1,0:T(8,128)(2,1)S(1)}, bf16[48,1536]{1,0:T(8,128)(2,1)S(1)}, u32[]{:S(2)}, u32[]{:S(2)}) collective-permute-start(bf16[48,1536]{1,0:T(8,128)(2,1)S(1)} %get-tuple-element.180), channel_id=1, source_target_pairs={{0,6},{1,7},{2,4},{3,5},{4,2},{5,3},{6,0},{7,1},{8,14},{9,15},{10,... | collective-permute-start | bytes 442376 | tf_op jit(solution)/shard_map/ppermute | solution.py:485
  413.3 12.8 %collective-permute-start.45 = (bf16[48,1536]{1,0:T(8,128)(2,1)S(1)}, bf16[48,1536]{1,0:T(8,128)(2,1)S(1)}, u32[]{:S(2)}, u32[]{:S(2)}) collective-permute-start(bf16[48,1536]{1,0:T(8,128)(2,1)S(1)} %get-tuple-element.179), channel_id=1, source_target_pairs={{0,4},{1,5},{2,6},{3,7},{4,0},{5,1},{6,2},{7,3},{8,12},{9,13},{10,... | collective-permute-start | bytes 442376 | tf_op jit(solution)/shard_map/ppermute | solution.py:485
  426.2 10.9 %collective-permute-start.47 = (bf16[48,1536]{1,0:T(8,128)(2,1)S(1)}, bf16[48,1536]{1,0:T(8,128)(2,1)S(1)}, u32[]{:S(2)}, u32[]{:S(2)}) collective-permute-start(bf16[48,1536]{1,0:T(8,128)(2,1)S(1)} %add_convert_fusion.10), channel_id=1, source_target_pairs={{0,16},{1,17},{2,18},{3,19},{4,20},{5,21},{6,22},{7,23},{8,24},{9,... | collective-permute-start | bytes 442376 | tf_op jit(solution)/shard_map/ppermute | solution.py:485
  437.2 9.5 %collective-permute-start.48 = (bf16[48,3072]{1,0:T(8,128)(2,1)S(1)}, bf16[48,3072]{1,0:T(8,128)(2,1)S(1)}, u32[]{:S(2)}, u32[]{:S(2)}) collective-permute-start(bf16[48,3072]{1,0:T(8,128)(2,1)S(1)} %pad_maximum_fusion.9), channel_id=1, source_target_pairs={{0,8},{1,9},{2,10},{3,11},{4,12},{5,13},{6,14},{7,15},{8,0},{9,1},... | collective-permute-start | bytes 884744 | tf_op jit(solution)/shard_map/ppermute | solution.py:485
  (47 other events, 522.4 us)
